TPU v7x, 32 devices: a whole 2x2x4 slice. The times are simulated.
32 devices in a mesh: mer: 8 (over z, y), az: 4 (over x, core).
Axes of the slice: x: 2, y: 2, z: 4, core: 2. Of those that a mesh axis runs over, the one named last changes fastest.
Arguments:
- displacement: float32 [3, 5, 64, 512], P(None, None, 'mer', 'az'), may hold values from -6 to 6
- velocity: float32 [3, 5, 64, 512], P(None, None, 'mer', 'az'), may hold values from -1.5 to 1.5
- modulus: float32 [1, 16], P(None, 'mer'), may hold values from 0.5 to 2
- hoop_strength: float32 [1, 16], P(None, 'mer'), may hold values from 0.5 to 2
- coupling: float32 [1, 16], P(None, 'mer'), may hold values from -1 to 1
- density: float32 [1, 16], P(None, 'mer'), may hold values from 0.5 to 2
- order_count: int32 [1, 16], P(None, 'mer'), may hold values from 1 to 256
- point_element: int32 [512, 2], P('mer'), may hold values from 0 to 15, as said below
- point_local: float32 [512, 2], P('mer'), may hold values from -1 to 1
- azimuth_scale: float32 [512], P('mer'), may hold values from 0.5 to 2
- point_owner: int32 [512, 1], P('mer'), may hold values from 0 to 7; in each aligned block of 64 rows (0 to 63, 64 to 127, ...) at most 16 rows name the same one
- point_cell: int32 [512], P('mer'), may hold values from 0 to 31
- adjoint_strain: float32 [9, 8, 32, 512], P(None, None, 'mer', 'az'), may hold values from -6 to 6
Outputs:
- final_displacement: float32 [3, 5, 64, 512], P(None, None, 'mer', 'az')
- kernel: float32 [8, 32, 512], P(None, 'mer', 'az')
Inputs may be any that keep to these rules, and one draw needn't show every extreme that they name: `point_element`: points p with p // 64 = i lie in colatitude elements i * 2 to (i + 1) * 2 - 1; the first column is below 1. `point_owner`: among the points of one device (aligned blocks of 64 points) no owner is named more than 16 times, a bound that some block reaches.
All inputs are finite; a program needn't handle non-finite values.
Results may differ from a plain program's by a relative error of at most 0.0003.
Values sent between devices are 32-bit elements; how exact they have to be, the bound alone decides.
A program may use at most 64 MiB of HBM per device.

v0:
```python
import math

import jax
import jax.numpy as jnp
import numpy as np
from jax import lax
from jax.sharding import PartitionSpec as P

ORDERS = 256
STEPS = 3


step_scale = 0.015
smooth_rate = 0.125


def from_behind(value, axis, steps):
    count = lax.axis_size(axis)
    first, last = (max(0, -steps), min(count, count - steps))
    return lax.ppermute(value, axis, [(source, source + steps) for source in range(first, last)])


def padded_2(array, sides, width):
    for axis, dim in sides:
        size, length = (lax.axis_size(axis), array.shape[dim])
        up = [(i, (i + 1) % size) for i in range(size)]
        down = [(j, i) for i, j in up]
        last = lax.slice_in_dim(array, length - width, length, axis=dim)
        first = lax.slice_in_dim(array, 0, width, axis=dim)
        before = lax.ppermute(last, axis, up)
        after = lax.ppermute(first, axis, down)
        array = jnp.concatenate([before, array, after], axis=dim)
    return array


def gll_tables():
    gll_nodes = np.array([-1.0, -math.sqrt(3.0 / 7.0), 0.0, math.sqrt(3.0 / 7.0), 1.0])
    gll_weights = np.array([0.1, 49.0 / 90.0, 32.0 / 45.0, 49.0 / 90.0, 0.1])
    derivative = np.zeros((5, 5))
    for i in range(5):
        for j in range(5):
            if i == j:
                derivative[i, j] = sum(
                    (1.0 / (gll_nodes[i] - gll_nodes[l]) for l in range(5) if l != i)
                )
            else:
                scale_i = np.prod([gll_nodes[i] - gll_nodes[l] for l in range(5) if l != i])
                scale_j = np.prod([gll_nodes[j] - gll_nodes[l] for l in range(5) if l != j])
                derivative[i, j] = scale_i / (scale_j * (gll_nodes[i] - gll_nodes[j]))
    return (gll_nodes, gll_weights, derivative)


def lagrange(position):
    gll_nodes = gll_tables()[0]
    basis_values = []
    basis_slopes = []
    for j in range(5):
        others = [l for l in range(5) if l != j]
        product = jnp.ones_like(position)
        for l in others:
            product = (
                product * (position - float(gll_nodes[l])) / float(gll_nodes[j] - gll_nodes[l])
            )
        gradient_sum = jnp.zeros_like(position)
        for l in others:
            summand = jnp.ones_like(position) / float(gll_nodes[j] - gll_nodes[l])
            for i in others:
                if i != l:
                    summand = (
                        summand
                        * (position - float(gll_nodes[i]))
                        / float(gll_nodes[j] - gll_nodes[i])
                    )
            gradient_sum = gradient_sum + summand
        basis_values.append(product)
        basis_slopes.append(gradient_sum)
    return (jnp.stack(basis_values, axis=1), jnp.stack(basis_slopes, axis=1))


def to_elements(nodal):
    count_rows = (nodal.shape[1] - 1) // 4
    count_cols = (nodal.shape[2] - 1) // 4
    radial = jnp.stack([nodal[:, a : a + 4 * count_rows : 4] for a in range(5)], axis=2)
    return jnp.stack([radial[:, :, :, b : b + 4 * count_cols : 4] for b in range(5)], axis=4)


def from_elements(element_values):
    components, count_rows, _, count_cols, _, coef_width = element_values.shape
    radial = jnp.zeros(
        (components, 4 * count_rows + 1, count_cols, 5, coef_width), element_values.dtype
    )
    for a in range(5):
        radial = radial.at[:, a : a + 4 * count_rows : 4].add(element_values[:, :, a])
    assembled = jnp.zeros(
        (components, 4 * count_rows + 1, 4 * count_cols + 1, coef_width), element_values.dtype
    )
    for b in range(5):
        assembled = assembled.at[:, :, b : b + 4 * count_cols : 4].add(radial[:, :, :, b])
    return assembled


def quadrature_table():
    gll_weights = jnp.asarray(gll_tables()[1], jnp.float32)
    return gll_weights[:, None] * gll_weights[None, :]


def rotate(vector, order_ratio):
    lane_index = lax.broadcasted_iota(jnp.int32, vector.shape, vector.ndim - 1)
    is_even = lane_index % 2 == 0
    return (
        jnp.where(is_even, jnp.roll(vector, -1, axis=-1), -jnp.roll(vector, 1, axis=-1))
        * order_ratio
    )


def element_mass(density):
    quadrature = quadrature_table()
    return (density[:, None, :, None] * quadrature[None, :, None, :])[None, :, :, :, :, None]


def element_forces(
    element_values, modulus, hoop_strength, coupling, order_count, order_index, order_ratio
):
    quadrature = quadrature_table()
    derivative = jnp.asarray(gll_tables()[2], jnp.float32)
    highest = lax.Precision.HIGHEST

    def spread(per_element):
        return (per_element[:, None, :, None] * quadrature[None, :, None, :])[:, :, :, :, None]

    stiff_node = spread(modulus)[None]
    hoop_node = spread(hoop_strength)[None]
    couple_node = spread(coupling)
    grad_radial = jnp.einsum("pa,cEaFbk->cEpFbk", derivative, element_values, precision=highest)
    grad_colat = jnp.einsum("qb,cEaFbk->cEaFqk", derivative, element_values, precision=highest)
    back_radial = jnp.einsum(
        "pa,cEpFbk->cEaFbk", derivative, stiff_node * grad_radial, precision=highest
    )
    back_colat = jnp.einsum(
        "qb,cEaFqk->cEaFbk", derivative, stiff_node * grad_colat, precision=highest
    )
    forces = -(back_radial + back_colat + hoop_node * (order_ratio * order_ratio) * element_values)
    forces = jnp.stack(
        [
            forces[0] + couple_node * rotate(element_values[2], order_ratio),
            forces[1],
            forces[2] - couple_node * rotate(element_values[0], order_ratio),
        ],
        axis=0,
    )
    order_mask = order_index[None, None, None, None, :] < order_count[:, None, :, None, None]
    return jnp.where(order_mask[None], forces, 0.0)


def point_gradients(
    gathered, xi_values, xi_slopes, eta_values, eta_slopes, azimuth_scale, order_ratio
):
    highest = lax.Precision.HIGHEST
    nodal_value = jnp.einsum("pa,pb,cpabk->pck", xi_values, eta_values, gathered, precision=highest)
    along_radius = jnp.einsum(
        "pa,pb,cpabk->pck", xi_slopes, eta_values, gathered, precision=highest
    )
    along_colat = jnp.einsum("pa,pb,cpabk->pck", xi_values, eta_slopes, gathered, precision=highest)
    around_axis = azimuth_scale[:, None, None] * rotate(nodal_value, order_ratio)
    stacked = jnp.stack([along_radius, along_colat, around_axis], axis=2)
    return stacked.reshape(gathered.shape[1], 9, gathered.shape[4])


def fourier_basis(coef_start, coef_count, phi_count, total_phi):
    coef_rows = coef_start + lax.broadcasted_iota(jnp.int32, (coef_count, phi_count), 0)
    phi_cols = lax.broadcasted_iota(jnp.int32, (coef_count, phi_count), 1)
    wrapped = coef_rows // 2 * phi_cols % total_phi
    angles = wrapped.astype(jnp.float32) * (2.0 * math.pi / total_phi)
    return jnp.where(coef_rows % 2 == 0, jnp.cos(angles), jnp.sin(angles))


def on_device(
    displacement,
    velocity,
    modulus,
    hoop_strength,
    coupling,
    density,
    order_count,
    point_element,
    point_local,
    azimuth_scale,
    point_owner,
    point_cell,
    adjoint_strain,
):
    highest = lax.Precision.HIGHEST
    coef_width = displacement.shape[3]
    local_cols = displacement.shape[2]
    elem_cols = modulus.shape[1]
    coef_first = lax.axis_index("az") * coef_width
    order_index = (coef_first + jnp.arange(coef_width, dtype=jnp.int32)) // 2
    order_ratio = order_index.astype(jnp.float32) / ORDERS
    mass_parts = from_elements(element_mass(density))
    mass_edge = from_behind(mass_parts[:, :, local_cols:], "mer", 1)
    nodal_mass = mass_parts[:, :, :local_cols].at[:, :, 0:1].add(mass_edge)[0]

    def right_rim(nodal):
        return from_behind(nodal[:, :, 0:1], "mer", -1)

    current = displacement
    previous = displacement - velocity
    for step_index in range(STEPS):
        padded = jnp.concatenate([current, right_rim(current)], axis=2)
        assembled = from_elements(
            element_forces(
                to_elements(padded),
                modulus,
                hoop_strength,
                coupling,
                order_count,
                order_index,
                order_ratio,
            )
        )
        incoming = from_behind(assembled[:, :, local_cols:], "mer", 1)
        forces = assembled[:, :, :local_cols].at[:, :, 0:1].add(incoming)
        following = 2.0 * current - previous + step_scale * forces / nodal_mass
        previous, current = (current, following)
    padded = jnp.concatenate([current, right_rim(current)], axis=2)
    xi_values, xi_slopes = lagrange(point_local[:, 0])
    eta_values, eta_slopes = lagrange(point_local[:, 1])
    offsets = jnp.arange(5, dtype=jnp.int32)[None, :]
    row_index = 4 * point_element[:, 0:1] + offsets
    col_index = 4 * (point_element[:, 1:2] % elem_cols) + offsets
    gathered = padded[:, row_index[:, :, None], col_index[:, None, :], :]
    gradients = point_gradients(
        gathered, xi_values, xi_slopes, eta_values, eta_slopes, azimuth_scale, order_ratio
    )
    point_count = gradients.shape[0]
    mer_count = lax.axis_size("mer")
    capacity = max(2, (2 * point_count + mer_count - 1) // mer_count)
    slot_total = mer_count * capacity
    owners = point_owner[:, 0]
    point_iota = jnp.arange(point_count, dtype=jnp.int32)
    earlier = (owners[None, :] == owners[:, None]) & (point_iota[None, :] < point_iota[:, None])
    slot_index = owners * capacity + jnp.sum(earlier.astype(jnp.int32), axis=1)
    placing = (slot_index[None, :] == jnp.arange(slot_total, dtype=jnp.int32)[:, None]).astype(
        jnp.float32
    )
    cell_code = jnp.dot(placing, (point_cell + 1).astype(jnp.float32), precision=highest) - 1.0
    outgoing = jnp.einsum("sp,pgk->sgk", placing, gradients, precision=highest)
    layer_count = adjoint_strain.shape[1]
    row_count_lat = adjoint_strain.shape[2]
    phi_width = adjoint_strain.shape[3]
    cell_total = layer_count * row_count_lat
    total_phi = 2 * ORDERS
    fourier_norm = 1.0 / math.sqrt(ORDERS)
    adjoint_cells = adjoint_strain.reshape(9, cell_total, phi_width)
    cell_iota = jnp.arange(cell_total, dtype=jnp.float32)
    arriving, arriving_cells = (
        lax.all_to_all(outgoing, "mer", split_axis=0, concat_axis=0, tiled=True),
        lax.all_to_all(cell_code, "mer", split_axis=0, concat_axis=0, tiled=True),
    )
    sorting = (arriving_cells[None, :] == cell_iota[:, None]).astype(jnp.float32)
    voxel_coefs = jnp.einsum("cs,sgk->cgk", sorting, arriving, precision=highest)
    basis = fourier_basis(coef_first, coef_width, phi_width * lax.axis_size("az"), total_phi)
    samples = (
        lax.psum_scatter(
            jnp.einsum("kj,cgk->jgc", basis, voxel_coefs, precision=highest),
            "az",
            scatter_dimension=0,
            tiled=True,
        )
        * fourier_norm
    )
    kernel_raw = jnp.einsum("jgc,gcj->cj", samples, adjoint_cells, precision=highest)
    kernel_block = kernel_raw.reshape(layer_count, row_count_lat, phi_width)
    framed = padded_2(kernel_block, (("mer", 1), ("az", 2)), 1)
    mer_index = lax.axis_index("mer")
    lower_keep = (mer_index > 0).astype(jnp.float32)
    upper_keep = (mer_index < mer_count - 1).astype(jnp.float32)
    lateral = jnp.concatenate(
        [framed[:, 0:1, 1:-1] * lower_keep, kernel_block, framed[:, -1:, 1:-1] * upper_keep], axis=1
    )
    neighbours = lateral[:, :-2] + lateral[:, 2:]
    neighbours = neighbours + framed[:, 1:-1, :-2] + framed[:, 1:-1, 2:]
    deeper = jnp.pad(kernel_block, ((1, 1), (0, 0), (0, 0)))
    neighbours = neighbours + deeper[2:] + deeper[:-2]
    kernel = kernel_block + smooth_rate * (neighbours - 6.0 * kernel_block)
    return (current, kernel)


def solution(mesh):
    placed = (
        P(None, None, "mer", "az"),
        P(None, None, "mer", "az"),
        P(None, "mer"),
        P(None, "mer"),
        P(None, "mer"),
        P(None, "mer"),
        P(None, "mer"),
        P("mer", None),
        P("mer", None),
        P("mer"),
        P("mer", None),
        P("mer"),
        P(None, None, "mer", "az"),
    )
    return jax.shard_map(
        on_device,
        mesh=mesh,
        in_specs=placed,
        out_specs=(P(None, None, "mer", "az"), P(None, "mer", "az")),
        check_vma=False,
    )
```

profile of v0, /device:TPU:0, one launch (start us, length us, event | category | flops | bytes accessed | tf_op | source)
XLA Modules:
  0.0 187.7 jit_solution(13464746163337977856)
XLA Ops:
  10.3 7.3 %all-to-all-start = ((f32[8,16,1]{1,2,0:T(1,128)}), f32[8,16,1]{1,2,0:T(1,128)S(1)}, u32[]{:S(2)}, u32[]{:S(2)}) async-start(f32[8,16,1]{1,2,0:T(1,128)} %bitcast.198), calls=%async_computation | async-start | bytes 8192 | tf_op jit(solution)/shard_map/all_to_all | solution.py:258
  23.0 3.9 %collective-permute-start.2 = (f32[1,5,1,1]{2,1,3,0:T(8,128)S(1)}, f32[1,5,1,1]{2,1,3,0:T(8,128)S(1)}, u32[]{:S(2)}, u32[]{:S(2)}) collective-permute-start(f32[1,5,1,1]{2,1,3,0:T(8,128)S(1)} %slice.1239), channel_id=1, source_target_pairs={{0,4},{4,8},{8,12},{12,16},{16,20},{20,24},{24,28},{1,5},{5,9},{9,... | collective-permute-start | bytes 68 | tf_op jit(solution)/shard_map/ppermute | solution.py:20
  27.8 1.3 collective-permute-start
  42.7 4.3 %collective-permute-start.1 = (f32[3,5,1,128]{3,1,2,0:T(8,128)S(1)}, f32[3,5,1,128]{3,1,2,0:T(8,128)S(1)}, u32[]{:S(2)}, u32[]{:S(2)}) collective-permute-start(f32[3,5,1,128]{3,1,2,0:T(8,128)S(1)} %copy.665), channel_id=1, source_target_pairs={{0,4},{4,8},{8,12},{12,16},{16,20},{20,24},{24,28},{1,5},{5,9},{9,... | collective-permute-start | bytes 23048 | tf_op jit(solution)/shard_map/ppermute | solution.py:20
  48.5 1.3 collective-permute-start.3
  50.3 4.0 %collective-permute-done.3 = f32[3,5,1,128]{3,1,2,0:T(8,128)S(1)} collective-permute-done((f32[3,5,1,128]{3,1,2,0:T(8,128)S(1)}, f32[3,5,1,128]{3,1,2,0:T(8,128)S(1)}, u32[]{:S(2)}, u32[]{:S(2)}) %collective-permute-start.3) | collective-permute-done | bytes 7712 | tf_op jit(solution)/shard_map/ppermute | solution.py:20
  61.6 4.8 %collective-permute-start.4 = (f32[3,5,1,128]{3,1,2,0:T(8,128)S(1)}, f32[3,5,1,128]{3,1,2,0:T(8,128)S(1)}, u32[]{:S(2)}, u32[]{:S(2)}) collective-permute-start(f32[3,5,1,128]{3,1,2,0:T(8,128)S(1)} %copy.672), channel_id=1, source_target_pairs={{0,4},{4,8},{8,12},{12,16},{16,20},{20,24},{24,28},{1,5},{5,9},{9,... | collective-permute-start | bytes 23048 | tf_op jit(solution)/shard_map/ppermute | solution.py:20
  67.9 1.3 collective-permute-start.5
  69.2 4.5 %collective-permute-done.5 = f32[3,5,1,128]{3,1,2,0:T(8,128)S(1)} collective-permute-done((f32[3,5,1,128]{3,1,2,0:T(8,128)S(1)}, f32[3,5,1,128]{3,1,2,0:T(8,128)S(1)}, u32[]{:S(2)}, u32[]{:S(2)}) %collective-permute-start.5) | collective-permute-done | bytes 7712 | tf_op jit(solution)/shard_map/ppermute | solution.py:20
  81.1 4.8 %collective-permute-start.6 = (f32[3,5,1,128]{3,1,2,0:T(8,128)S(1)}, f32[3,5,1,128]{3,1,2,0:T(8,128)S(1)}, u32[]{:S(2)}, u32[]{:S(2)}) collective-permute-start(f32[3,5,1,128]{3,1,2,0:T(8,128)S(1)} %copy.679), channel_id=1, source_target_pairs={{0,4},{4,8},{8,12},{12,16},{16,20},{20,24},{24,28},{1,5},{5,9},{9,... | collective-permute-start | bytes 23048 | tf_op jit(solution)/shard_map/ppermute | solution.py:20
  87.4 1.3 collective-permute-start.7
  93.3 11.0 %gather_fusion = f32[1600,3,128]{2,1,0:T(4,128)S(1)} fusion(f32[3,5,9,128]{3,0,2,1:T(4,128)S(1)} %copy.619, s32[1600]{0:T(1024)S(1)} %reshape.2300), kind=kCustom, calls=%fused_computation | custom fusion | bytes 4928000 | tf_op jit(solution)/shard_map/gather | solution.py:231
  104.3 4.4 %fusion = f32[64,1,3,128,1]{3,1,4,2,0:T(1,128)S(1)} fusion(f32[64,5,5,1,1]{1,3,2,4,0:T(1,128)} %copy.643, f32[64,5,5,3,128]{4,3,2,1,0:T(4,128)S(1)} %bitcast.575), kind=kOutput, calls=%fused_computation.21 | convolution fusion | flops 7372800 | bytes 2562304 | tf_op jit(solution)/shard_map/pa,pb,cpabk->pck/dot_general | solution.py:159
  109.0 3.5 %fusion.2 = f32[64,1,3,128,1]{3,1,4,2,0:T(1,128)S(1)} fusion(f32[64,5,5,1,1]{1,3,2,4,0:T(1,128)S(1)} %copy-done.1, f32[64,5,5,3,128]{4,3,2,1,0:T(4,128)S(1)} %bitcast.576), kind=kOutput, calls=%fused_computation.23 | convolution fusion | flops 7372800 | bytes 2562304 | tf_op jit(solution)/shard_map/pa,pb,cpabk->pck/dot_general | solution.py:163
  112.5 3.5 %fusion.4 = f32[64,1,3,128,1]{3,1,4,2,0:T(1,128)S(1)} fusion(f32[64,5,5,1,1]{1,3,2,4,0:T(1,128)S(1)} %copy-done, f32[64,5,5,3,128]{4,3,2,1,0:T(4,128)S(1)} %bitcast.577), kind=kOutput, calls=%fused_computation.25 | convolution fusion | flops 7372800 | bytes 2562304 | tf_op jit(solution)/shard_map/pa,pb,cpabk->pck/dot_general | solution.py:160
  116.7 1.4 copy.628
  118.1 8.0 %all-to-all-start.1 = ((f32[128,9,128]{2,1,0:T(8,128)}), f32[128,9,128]{2,1,0:T(8,128)S(1)}, u32[]{:S(2)}, u32[]{:S(2)}) async-start(f32[128,9,128]{2,1,0:T(8,128)} %copy.628), calls=%async_computation.1 | async-start | bytes 2097152 | tf_op jit(solution)/shard_map/all_to_all | solution.py:257
  127.7 17.5 %all-to-all-done.1 = f32[128,9,128]{2,1,0:T(8,128)S(1)} async-done(((f32[128,9,128]{2,1,0:T(8,128)}), f32[128,9,128]{2,1,0:T(8,128)S(1)}, u32[]{:S(2)}, u32[]{:S(2)}) %all-to-all-start.1) | async-done | bytes 589856 | tf_op jit(solution)/shard_map/all_to_all | solution.py:257
  145.6 2.6 %convolution_bitcast_fusion = f32[512,9,32]{0,2,1:T(8,128)} fusion(f32[32,9,128]{2,0,1:T(8,128)S(1)} %fusion.31, s32[128]{0:T(128)S(1)} %get-tuple-element.421, s32[128]{0:T(128)S(1)} %get-tuple-element.426, s32[128]{0:T(128)S(1)} %get-tuple-element.422, s32[128]{0:T(128)S(1)} %get-tuple-element.425, pred[128]{0:T(512)(128)(4,1)S(1)} %get-tuple-element.420, ...), kind=kOutput, calls=%fused_computation.30 | convolution fusion | flops 227672064 | bytes 739584 | tf_op jit(solution)/shard_map/kj,cgk->jgc/dot_general | solution.py:265
  148.2 21.1 %reduce-scatter.2.cloned.1.call-done = f32[128,9,32]{0,2,1:T(8,128)} async-done(((f32[512,9,32]{0,2,1:T(8,128)}), f32[128,9,32]{0,2,1:T(8,128)}) %reduce-scatter.2.cloned.1.call-update) | async-done | bytes 147472 | tf_op jit(solution)/shard_map/reduce_scatter | solution.py:264
  170.3 1.5 collective-permute-start.8
  171.8 3.2 %collective-permute-start.9 = (f32[8,1,128]{2,1,0:T(1,128)S(1)}, f32[8,1,128]{2,1,0:T(1,128)S(1)}, u32[]{:S(2)}, u32[]{:S(2)}) collective-permute-start(f32[8,1,128]{2,1,0:T(1,128)S(1)} %get-tuple-element.389), channel_id=1, source_target_pairs={{4,0},{8,4},{12,8},{16,12},{20,16},{24,20},{28,24},{0,28},{5,1},{9... | collective-permute-start | bytes 12296 | tf_op jit(solution)/shard_map/ppermute | solution.py:31
  176.7 1.7 collective-permute-start.11
  178.5 1.6 collective-permute-done.10
  (287 shorter events, 52.3 us)
Async XLA Ops:
  7.2 31.0 %copy-start.3 = (f32[5,5,1,1,1]{1,0,4,3,2:T(8,128)S(1)}, f32[5,5,1,1,1]{1,0,4,3,2:T(8,128)}, u32[]{:S(2)}) copy-start(f32[5,5,1,1,1]{1,0,4,3,2:T(8,128)} %constant.924) | copy-start | bytes 304
  7.2 41.2 %copy-start.2 = (f32[3,5,8,128]{3,2,1,0:T(8,128)S(1)}, f32[3,5,8,128]{3,2,1,0:T(8,128)}, u32[]{:S(2)}) copy-start(f32[3,5,8,128]{3,2,1,0:T(8,128)} %param.68) | copy-start | bytes 184324
  7.2 41.2 %copy-start.5 = (f32[3,5,8,128]{3,2,1,0:T(8,128)S(1)}, f32[3,5,8,128]{3,2,1,0:T(8,128)}, u32[]{:S(2)}) copy-start(f32[3,5,8,128]{3,2,1,0:T(8,128)} %param.69) | copy-start | bytes 184324
  10.3 107.8 %all-to-all-start = ((f32[8,16,1]{1,2,0:T(1,128)}), f32[8,16,1]{1,2,0:T(1,128)S(1)}, u32[]{:S(2)}, u32[]{:S(2)}) async-start(f32[8,16,1]{1,2,0:T(1,128)} %bitcast.198), calls=%async_computation | async-start | bytes 8192 | tf_op jit(solution)/shard_map/all_to_all | solution.py:258
  19.5 30.2 %copy-start.7 = (f32[64,2]{0,1:T(2,128)S(1)}, f32[64,2]{0,1:T(2,128)}, u32[]{:S(2)}) copy-start(f32[64,2]{0,1:T(2,128)} %param.76) | copy-start | bytes 1540
  23.0 23.9 %collective-permute-start.2 = (f32[1,5,1,1]{2,1,3,0:T(8,128)S(1)}, f32[1,5,1,1]{2,1,3,0:T(8,128)S(1)}, u32[]{:S(2)}, u32[]{:S(2)}) collective-permute-start(f32[1,5,1,1]{2,1,3,0:T(8,128)S(1)} %slice.1239), channel_id=1, source_target_pairs={{0,4},{4,8},{8,12},{12,16},{16,20},{20,24},{24,28},{1,5},{5,9},{9,... | collective-permute-start | bytes 68 | tf_op jit(solution)/shard_map/ppermute | solution.py:20
  27.8 5.6 %collective-permute-start = (f32[3,5,1,128]{3,1,2,0:T(8,128)S(1)}, f32[3,5,1,128]{3,1,2,0:T(8,128)S(1)}, u32[]{:S(2)}, u32[]{:S(2)}) collective-permute-start(f32[3,5,1,128]{3,1,2,0:T(8,128)S(1)} %copy.728), channel_id=1, source_target_pairs={{4,0},{8,4},{12,8},{16,12},{20,16},{24,20},{28,24},{5,1},{9,5},{13... | collective-permute-start | bytes 23048 | tf_op jit(solution)/shard_map/ppermute | solution.py:20
  42.7 5.7 %collective-permute-start.1 = (f32[3,5,1,128]{3,1,2,0:T(8,128)S(1)}, f32[3,5,1,128]{3,1,2,0:T(8,128)S(1)}, u32[]{:S(2)}, u32[]{:S(2)}) collective-permute-start(f32[3,5,1,128]{3,1,2,0:T(8,128)S(1)} %copy.665), channel_id=1, source_target_pairs={{0,4},{4,8},{8,12},{12,16},{16,20},{20,24},{24,28},{1,5},{5,9},{9,... | collective-permute-start | bytes 23048 | tf_op jit(solution)/shard_map/ppermute | solution.py:20
  48.5 5.9 %collective-permute-start.3 = (f32[3,5,1,128]{3,1,2,0:T(8,128)S(1)}, f32[3,5,1,128]{3,1,2,0:T(8,128)S(1)}, u32[]{:S(2)}, u32[]{:S(2)}) collective-permute-start(f32[3,5,1,128]{3,1,2,0:T(8,128)S(1)} %slice.1389), channel_id=1, source_target_pairs={{4,0},{8,4},{12,8},{16,12},{20,16},{24,20},{28,24},{5,1},{9,5},{13... | collective-permute-start | bytes 23048 | tf_op jit(solution)/shard_map/ppermute | solution.py:20
  54.5 14.7 %copy-start.6 = (s32[64,2]{0,1:T(2,128)S(1)}, s32[64,2]{0,1:T(2,128)}, u32[]{:S(2)}) copy-start(s32[64,2]{0,1:T(2,128)} %param.75) | copy-start | bytes 1540
  61.6 6.2 %collective-permute-start.4 = (f32[3,5,1,128]{3,1,2,0:T(8,128)S(1)}, f32[3,5,1,128]{3,1,2,0:T(8,128)S(1)}, u32[]{:S(2)}, u32[]{:S(2)}) collective-permute-start(f32[3,5,1,128]{3,1,2,0:T(8,128)S(1)} %copy.672), channel_id=1, source_target_pairs={{0,4},{4,8},{8,12},{12,16},{16,20},{20,24},{24,28},{1,5},{5,9},{9,... | collective-permute-start | bytes 23048 | tf_op jit(solution)/shard_map/ppermute | solution.py:20
  67.9 5.9 %collective-permute-start.5 = (f32[3,5,1,128]{3,1,2,0:T(8,128)S(1)}, f32[3,5,1,128]{3,1,2,0:T(8,128)S(1)}, u32[]{:S(2)}, u32[]{:S(2)}) collective-permute-start(f32[3,5,1,128]{3,1,2,0:T(8,128)S(1)} %slice.1419), channel_id=1, source_target_pairs={{4,0},{8,4},{12,8},{16,12},{20,16},{24,20},{28,24},{5,1},{9,5},{13... | collective-permute-start | bytes 23048 | tf_op jit(solution)/shard_map/ppermute | solution.py:20
  81.1 6.2 %collective-permute-start.6 = (f32[3,5,1,128]{3,1,2,0:T(8,128)S(1)}, f32[3,5,1,128]{3,1,2,0:T(8,128)S(1)}, u32[]{:S(2)}, u32[]{:S(2)}) collective-permute-start(f32[3,5,1,128]{3,1,2,0:T(8,128)S(1)} %copy.679), channel_id=1, source_target_pairs={{0,4},{4,8},{8,12},{12,16},{16,20},{20,24},{24,28},{1,5},{5,9},{9,... | collective-permute-start | bytes 23048 | tf_op jit(solution)/shard_map/ppermute | solution.py:20
  87.4 5.9 %collective-permute-start.7 = (f32[3,5,1,128]{3,1,2,0:T(8,128)S(1)}, f32[3,5,1,128]{3,1,2,0:T(8,128)S(1)}, u32[]{:S(2)}, u32[]{:S(2)}) collective-permute-start(f32[3,5,1,128]{3,1,2,0:T(8,128)S(1)} %slice.1449), channel_id=1, source_target_pairs={{4,0},{8,4},{12,8},{16,12},{20,16},{24,20},{28,24},{5,1},{9,5},{13... | collective-permute-start | bytes 23048 | tf_op jit(solution)/shard_map/ppermute | solution.py:20
  104.3 4.7 %copy-start.1 = (f32[64,5,5,1,1]{1,3,2,4,0:T(1,128)S(1)}, f32[64,5,5,1,1]{1,3,2,4,0:T(1,128)}, u32[]{:S(2)}) copy-start(f32[64,5,5,1,1]{1,3,2,4,0:T(1,128)} %copy.641) | copy-start | bytes 19204
  108.8 3.7 %copy-start = (f32[64,5,5,1,1]{1,3,2,4,0:T(1,128)S(1)}, f32[64,5,5,1,1]{1,3,2,4,0:T(1,128)}, u32[]{:S(2)}) copy-start(f32[64,5,5,1,1]{1,3,2,4,0:T(1,128)} %copy.639) | copy-start | bytes 19204
  112.5 3.5 %copy-start.8 = (f32[64]{0:T(128)S(1)}, f32[64]{0:T(128)}, u32[]{:S(2)}) copy-start(f32[64]{0:T(128)} %param.77) | copy-start | bytes 772
  116.7 52.6 %copy-start.4 = (f32[9,8,4,128]{3,2,1,0:T(4,128)S(1)}, f32[9,8,4,128]{3,2,1,0:T(4,128)}, u32[]{:S(2)}) copy-start(f32[9,8,4,128]{3,2,1,0:T(4,128)} %param.80) | copy-start | bytes 442372
  118.1 27.1 %all-to-all-start.1 = ((f32[128,9,128]{2,1,0:T(8,128)}), f32[128,9,128]{2,1,0:T(8,128)S(1)}, u32[]{:S(2)}, u32[]{:S(2)}) async-start(f32[128,9,128]{2,1,0:T(8,128)} %copy.628), calls=%async_computation.1 | async-start | bytes 2097152 | tf_op jit(solution)/shard_map/all_to_all | solution.py:257
  126.1 43.2 %reduce-scatter.2.cloned.1.call-start = ((), (), s32[]{:S(2)}) async-start(), calls=%async_computation.3 | async-start | bytes 737280 | tf_op jit(solution)/shard_map/reduce_scatter | solution.py:264
  170.3 6.4 %collective-permute-start.8 = (f32[8,1,128]{2,1,0:T(1,128)S(1)}, f32[8,1,128]{2,1,0:T(1,128)S(1)}, u32[]{:S(2)}, u32[]{:S(2)}) collective-permute-start(f32[8,1,128]{2,1,0:T(1,128)S(1)} %get-tuple-element.388), channel_id=1, source_target_pairs={{0,4},{4,8},{8,12},{12,16},{16,20},{20,24},{24,28},{28,0},{1,5},{5... | collective-permute-start | bytes 12296 | tf_op jit(solution)/shard_map/ppermute | solution.py:30
  171.8 4.8 %collective-permute-start.9 = (f32[8,1,128]{2,1,0:T(1,128)S(1)}, f32[8,1,128]{2,1,0:T(1,128)S(1)}, u32[]{:S(2)}, u32[]{:S(2)}) collective-permute-start(f32[8,1,128]{2,1,0:T(1,128)S(1)} %get-tuple-element.389), channel_id=1, source_target_pairs={{4,0},{8,4},{12,8},{16,12},{20,16},{24,20},{28,24},{0,28},{5,1},{9... | collective-permute-start | bytes 12296 | tf_op jit(solution)/shard_map/ppermute | solution.py:31
  176.7 3.3 %collective-permute-start.10 = (f32[8,6,1]{2,1,0:T(8,128)S(1)}, f32[8,6,1]{2,1,0:T(8,128)S(1)}, u32[]{:S(2)}, u32[]{:S(2)}) collective-permute-start(f32[8,6,1]{2,1,0:T(8,128)S(1)} %get-tuple-element.383), channel_id=1, source_target_pairs={{0,1},{1,2},{2,3},{3,0},{4,5},{5,6},{6,7},{7,4},{8,9},{9,10},{10,1... | collective-permute-start | bytes 584 | tf_op jit(solution)/shard_map/ppermute | solution.py:30
  176.7 3.3 %collective-permute-start.11 = (f32[8,6,1]{2,1,0:T(8,128)S(1)}, f32[8,6,1]{2,1,0:T(8,128)S(1)}, u32[]{:S(2)}, u32[]{:S(2)}) collective-permute-start(f32[8,6,1]{2,1,0:T(8,128)S(1)} %get-tuple-element.384), channel_id=1, source_target_pairs={{1,0},{2,1},{3,2},{0,3},{5,4},{6,5},{7,6},{4,7},{9,8},{10,9},{11,1... | collective-permute-start | bytes 584 | tf_op jit(solution)/shard_map/ppermute | solution.py:31
Sparse Core Ops, SparseCore 0:
  148.3 20.9 reduce-scatter.1
where the time goes:
time: 188 us
  waiting for transfers between devices  54.8 us (29%)
  starting transfers between devices  45 us (24%)
  local copies, waits for them, and re-layouts  28.5 us (15%)
  other arithmetic  22.6 us (12%)
  matrix products  21.3 us (11%)
  between operations  15.5 us (8%)
    ppermute x8, starting transfers between devices, from_behind(): lax.ppermute(value, axis, [(source, source + steps) for source in range(f...  23 us
    reduce_scatter x1, waiting for transfers between devices, on_device(): lax.psum_scatter(jnp.einsum('kj,cgk->jgc', basis, voxel_coefs, precision=...  21.1 us
    all_to_all x1, waiting for transfers between devices, on_device(): lax.all_to_all(outgoing, 'mer', split_axis=0, concat_axis=0, tiled=True)  17.5 us
    ppermute x8, waiting for transfers between devices, from_behind(): lax.ppermute(value, axis, [(source, source + steps) for source in range(f...  13.7 us
    scatter-add x20, other arithmetic, from_elements(): assembled.at[:, :, b:b + 4 * count_cols:4].add(radial[:, :, :, b])  12.9 us
    gather x1, local copies, waits for them, and re-layouts, on_device(): gathered = padded[:, row_index[:, :, None], col_index[:, None, :], :]  11 us
    all_to_all x1, starting transfers between devices, on_device(): lax.all_to_all(outgoing, 'mer', split_axis=0, concat_axis=0, tiled=True)  8.01 us
    all_to_all x1, starting transfers between devices, on_device(): lax.all_to_all(cell_code, 'mer', split_axis=0, concat_axis=0, tiled=True)  7.28 us
  transfers between devices with their start and end apart: 15, of which 11 were waited for; matrix products, arithmetic and copies ran while one was open for 34% of the time, Pallas kernels for 0%

commit v1 on v0

v1 whole, which is shorter than its diff:
```python
import functools
import math

import jax
import jax.numpy as jnp
import ml_dtypes
import numpy as np
from jax import lax
from jax.experimental import pallas as pl
from jax.experimental.pallas import tpu as pltpu
from jax.sharding import PartitionSpec as P

ORDERS = 256
STEPS = 3
step_scale = 0.015
smooth_rate = 0.125
MESH = pl.DeviceIdType.MESH


def gll_tables():
    nodes = np.array([-1.0, -math.sqrt(3.0 / 7.0), 0.0, math.sqrt(3.0 / 7.0), 1.0])
    weights = np.array([0.1, 49.0 / 90.0, 32.0 / 45.0, 49.0 / 90.0, 0.1])
    monomials = np.zeros((5, 5))
    for j in range(5):
        poly = np.array([1.0])
        for l in range(5):
            if l != j:
                poly = np.convolve(poly, np.array([1.0, -nodes[l]]) / (nodes[j] - nodes[l]))
        monomials[j] = poly[::-1]
    slopes = monomials[:, 1:] * np.arange(1, 5)
    derivative = np.array(
        [[sum(slopes[j, p] * nodes[i] ** p for p in range(4)) for j in range(5)] for i in range(5)]
    )
    stiffness = derivative.T @ np.diag(weights) @ derivative
    return weights, monomials, slopes, stiffness


def lane_table(elements, cols, lanes):
    _, monomials, slopes, _ = gll_tables()
    table = np.zeros((9 * (1 + elements), lanes), np.float32)
    for lane in range(lanes):
        half, spot = divmod(lane, lanes // 2)
        a, col = divmod(spot, cols)
        if a > 4 or (half and col):
            continue
        col = cols if half else col
        table[0:5, lane], table[5:9, lane] = monomials[a], slopes[a]
        for e in range(elements):
            b = col - 4 * e
            if 0 <= b <= 4:
                at = 9 * (1 + e)
                table[at : at + 5, lane], table[at + 5 : at + 9, lane] = monomials[b], slopes[b]
    return table


def column_table(elements, cols, lanes):
    weights, _, _, stiffness = gll_tables()
    table = np.zeros((elements, cols + 2, cols, lanes), np.float32)
    for e in range(elements):
        for c in range(cols):
            b = c - 4 * e
            if not 0 <= b <= 4:
                continue
            table[e, 0, c] = weights[b]
            for d in range(cols):
                other = (c - d) % cols - 4 * e
                if 0 <= other <= 4:
                    table[e, 1 + d, c] = stiffness[b, other]
            if cols - 4 * e == 4:
                table[e, cols + 1, c] = stiffness[b, 4]
    return table


def rim_table(cols, lanes):
    _, _, _, stiffness = gll_tables()
    table = np.zeros((cols, cols, lanes), np.float32)
    for d in range(cols):
        for a in range(5):
            other = (a - d) % cols
            if other <= 4:
                table[d, a] = stiffness[a, other]
    return table


def basis_tables(az_count, width, phi_width):
    coefs, phis = az_count * width, az_count * phi_width
    k, j = np.arange(coefs)[:, None], np.arange(phis)[None, :]
    angles = (k // 2) * j % (2 * ORDERS) * (2.0 * math.pi / (2 * ORDERS))
    basis = np.where(k % 2 == 0, np.cos(angles), np.sin(angles)) / math.sqrt(ORDERS)
    basis = basis.reshape(az_count, width, az_count, phi_width).transpose(0, 2, 1, 3)
    basis = basis.astype(np.float32)
    high = basis.astype(ml_dtypes.bfloat16)
    low = (basis - high.astype(np.float32)).astype(ml_dtypes.bfloat16)
    return high, low


def halves(x):
    high = x.astype(jnp.bfloat16)
    return high, (x - high.astype(jnp.float32)).astype(jnp.bfloat16)


def dot(x, y):
    return jnp.dot(x, y, preferred_element_type=jnp.float32)


def dot3(x, y):
    (xh, xl), (yh, yl) = x, y
    return dot(xh, yh) + (dot(xl, yh) + dot(xh, yl))


def kernel(
    n, az, disp, vel, modulus, hoop, coupling, density, orders, element, local, scale, owner, cell,
    adjoint, bhi, blo, lanes_t, cols_t, rim_t, out_u, out_k,
    halo_out, halo_in, dens_out, dens_in, fl_out, fr_out, fl_in, fr_in, meta, gathered, mix,
    adj_all, bh, bl, part_out, part_in, face_out, face_in,
    halo_s, halo_r, dens_s, dens_r, f_s, f_r, meta_s, meta_r, adj_s, adj_r, ga_s, ga_r, gb_s, gb_r,
    part_s, part_r, face_s, face_r, b_s,
):
    o, q = lax.axis_index("mer"), lax.axis_index("az")
    comps, nr, cols, width = disp.shape
    elements = modulus.shape[1]
    points = owner.shape[0]
    slot = gathered.shape[2]
    nodes = nr * cols
    cells = adjoint.shape[1]
    depth = face_in.shape[2]
    weights, _, _, stiffness = gll_tables()
    has_left, has_right = o > 0, o < n - 1

    halo_in[...] = jnp.zeros_like(halo_in)
    dens_in[...] = jnp.zeros_like(dens_in)
    fl_in[...] = jnp.zeros_like(fl_in)
    fr_in[...] = jnp.zeros_like(fr_in)
    face_in[...] = jnp.zeros_like(face_in)
    gathered[:, :, nodes:, :] = jnp.zeros((n, comps, slot - nodes, width), jnp.float32)

    barrier = pltpu.get_barrier_semaphore()

    @pl.loop(1, n)
    def _(h):
        pl.semaphore_signal(barrier, inc=1, device_id=(lax.rem(o + h, n), q), device_id_type=MESH)

    for h in range(1, az):
        r = lax.rem(q + h, az)
        pl.semaphore_signal(barrier, inc=1, device_id=(o, r), device_id_type=MESH)

        @pl.when(has_left)
        def _():
            pl.semaphore_signal(barrier, inc=1, device_id=(o - 1, r), device_id_type=MESH)

        @pl.when(has_right)
        def _():
            pl.semaphore_signal(barrier, inc=1, device_id=(o + 1, r), device_id_type=MESH)

    basis_copies = [
        pltpu.make_async_copy(bhi.at[q], bh, b_s.at[0]),
        pltpu.make_async_copy(blo.at[q], bl, b_s.at[1]),
    ]
    for copy in basis_copies:
        copy.start()

    row = lax.broadcasted_iota(jnp.int32, (cols, width), 0)
    lane = lax.broadcasted_iota(jnp.int32, (1, width), 1)
    u = [disp[:, a] for a in range(nr)]
    v = [vel[:, a] for a in range(nr)]

    def first_column(values):
        total = jnp.zeros((comps, cols, width), jnp.float32)
        for a in range(nr):
            total = jnp.where((row == a)[None], values[a][:, 0:1, :], total)
        return total

    halo_out[0:comps] = first_column(u)
    halo_out[comps : 2 * comps] = first_column(v)
    halo_out[2 * comps] = jnp.full((cols, width), density[0, 0])
    dens_out[...] = jnp.full((cols, width), density[0, elements - 1])
    eye = lax.broadcasted_iota(jnp.int32, (points, width), 0) == lax.broadcasted_iota(
        jnp.int32, (points, width), 1
    )

    def as_row(column):
        return jnp.sum(jnp.where(eye, column, 0.0), axis=0, keepdims=True)

    def as_column(line):
        return jnp.sum(jnp.where(eye, line, 0.0), axis=1, keepdims=True)

    spare = jnp.zeros((1, width - points), jnp.float32) if width > points else None

    def wide(line):
        return line if spare is None else jnp.concatenate([line, spare], axis=1)

    meta[o] = jnp.concatenate(
        [
            as_row(local[:, 0:1]),
            as_row(local[:, 1:2]),
            as_row((element[:, 1:2] % elements).astype(jnp.float32)),
            as_row(owner[:, 0:1].astype(jnp.float32)),
            wide(scale[...]),
            wide(cell[...].astype(jnp.float32)),
            jnp.zeros((2, width), jnp.float32),
        ],
        axis=0,
    )

    pl.semaphore_wait(
        barrier,
        n - 1 + (az - 1) * (1 + has_left.astype(jnp.int32) + has_right.astype(jnp.int32)),
    )

    def remote(src, dst, send, recv, device):
        return pltpu.make_async_remote_copy(
            src_ref=src, dst_ref=dst, send_sem=send, recv_sem=recv,
            device_id=device, device_id_type=MESH,
        )

    to_left = lambda: remote(halo_out, halo_in, halo_s, halo_r, (o - 1, q))
    to_right = lambda: remote(dens_out, dens_in, dens_s, dens_r, (o + 1, q))
    pl.when(has_left)(lambda: to_left().start())
    pl.when(has_right)(lambda: to_right().start())

    def meta_copy(h):
        return remote(meta.at[o], meta.at[o], meta_s.at[h], meta_r.at[h], (lax.rem(o + h, n), q))

    pl.loop(1, n)(lambda h: meta_copy(h).start())

    def adj_copy(h):
        return remote(
            adjoint, adj_all.at[h], adj_s.at[h], adj_r.at[h], (o, lax.rem(q + az - h, az))
        )

    for h in range(1, az):
        adj_copy(h).start()

    order = (q * width + lane) // 2
    ratio = order.astype(jnp.float32) / ORDERS
    even = (lane % 2 == 0)
    keep = [jnp.where(order < orders[0, e], 1.0, 0.0) for e in range(elements)]
    mod = [modulus[0, e] * keep[e] for e in range(elements)]
    hp = [hoop[0, e] * keep[e] * (ratio * ratio) for e in range(elements)]
    cp = [coupling[0, e] * keep[e] * ratio for e in range(elements)]
    last = elements - 1
    w_end = float(weights[4])

    def blend(per_element, which):
        total = per_element[0] * cols_t[0, which]
        for e in range(1, elements):
            total = total + per_element[e] * cols_t[e, which]
        return total

    c_radial, c_hoop, c_pair = blend(mod, 0), blend(hp, 0), blend(cp, 0)
    c_colat = [blend(mod, 1 + d) for d in range(cols)]
    c_rim = mod[last] * cols_t[last, cols + 1]
    w_rim = jnp.zeros((cols, width), jnp.float32)
    for a in range(nr):
        w_rim = jnp.where(row == a, float(weights[a]), w_rim)
    r_radial = [mod[last] * w_end * rim_t[d] for d in range(cols)]
    r_radial[0] = r_radial[0] + w_rim * (
        mod[last] * float(stiffness[4, 4]) + hp[last] * w_end
    )
    r_pair = w_rim * (cp[last] * w_end)

    pl.when(has_left)(lambda: to_left().wait_send())
    pl.when(has_right)(lambda: to_right().wait_send())
    pl.when(has_right)(lambda: to_left().wait_recv())
    pl.when(has_left)(lambda: to_right().wait_recv())
    col_mass = density[0, 0] * cols_t[0, 0]
    for e in range(1, elements):
        col_mass = col_mass + density[0, e] * cols_t[e, 0]
    col_mass = col_mass + jnp.where(row == 0, w_end * dens_in[...], 0.0)
    rim_mass = w_end * (density[0, last] + halo_in[2 * comps])
    inv_main = [step_scale / (float(weights[a]) * col_mass) for a in range(nr)]
    inv_rim = step_scale / (jnp.where(row < nr, w_rim, 1.0) * rim_mass)
    inv_rim = jnp.where(has_right, inv_rim, 0.0)

    rim = halo_in[0:comps]
    rim_before = rim - halo_in[comps : 2 * comps]
    before = [u[a] - v[a] for a in range(nr)]

    def swap(x):
        axis = x.ndim - 1
        return jnp.where(even, pltpu.roll(x, width - 1, axis), -pltpu.roll(x, 1, axis))

    def pair(x, factor):
        return jnp.stack(
            [factor * swap(x[2]), jnp.zeros((cols, width), jnp.float32), -factor * swap(x[0])]
        )

    def left_force(step):
        return remote(fl_out.at[step], fr_in.at[step], f_s.at[0, step], f_r.at[0, step], (o - 1, q))

    def right_force(step):
        return remote(fr_out.at[step], fl_in.at[step], f_s.at[1, step], f_r.at[1, step], (o + 1, q))

    for step in range(STEPS):
        forces, rim_force = [], jnp.zeros((comps, cols, width), jnp.float32)
        for a in range(nr):
            w_a = float(weights[a])
            colat = c_rim * rim[:, a : a + 1, :] + c_colat[0] * u[a]
            for d in range(1, cols):
                colat = colat + c_colat[d] * pltpu.roll(u[a], d, 1)
            radial = float(stiffness[a, 0]) * u[0]
            for i in range(1, nr):
                radial = radial + float(stiffness[a, i]) * u[i]
            force = pair(u[a], w_a * c_pair) - (
                c_radial * radial + w_a * (colat + c_hoop * u[a])
            )
            forces.append(force)
            ending = jnp.sum(c_rim * u[a], axis=1, keepdims=True)
            rim_force = jnp.where((row == a)[None], -w_a * ending, rim_force)
        rim_force = rim_force + pair(rim, r_pair)
        for d in range(cols):
            rim_force = rim_force - r_radial[d] * (pltpu.roll(rim, d, 1) if d else rim)
        fl_out[step] = first_column(forces)
        fr_out[step] = rim_force
        pl.when(has_left)(lambda: left_force(step).start())
        pl.when(has_right)(lambda: right_force(step).start())
        ahead = [2.0 * u[a] - before[a] + inv_main[a] * forces[a] for a in range(nr)]
        if step == 0:
            pl.loop(1, n)(lambda h: meta_copy(h).wait_send())
            pl.loop(1, n)(lambda h: meta_copy(h).wait_recv())
            mix[...] = jnp.zeros_like(mix)
            wanted = lax.broadcasted_iota(jnp.int32, (cells, points), 0)
            wanted = ((wanted % depth) * (cells // depth) + wanted // depth).astype(jnp.float32)
            upper = lane >= slot

            def horner(x, at, count):
                total = lanes_t[at + count - 1 : at + count, :]
                for p in range(count - 2, -1, -1):
                    total = total * x + lanes_t[at + p : at + p + 1, :]
                return total

            def block_mix(i):
                xi, eta = as_column(meta[i, 0:1, :]), as_column(meta[i, 1:2, :])
                spot, factor = as_column(meta[i, 2:3, :]), as_column(meta[i, 4:5, :])
                xi = jnp.broadcast_to(xi, (points, width))
                eta = jnp.broadcast_to(eta, (points, width))
                l_xi, s_xi = horner(xi, 0, 5), horner(xi, 5, 4)
                l_eta, s_eta = horner(eta, 9, 5), horner(eta, 14, 4)
                for e in range(1, elements):
                    here = spot == float(e)
                    l_eta = jnp.where(here, horner(eta, 9 + 9 * e, 5), l_eta)
                    s_eta = jnp.where(here, horner(eta, 14 + 9 * e, 4), s_eta)
                mine = meta[i, 3:4, 0:points] == o.astype(jnp.float32)
                chosen = jnp.where(mine & (meta[i, 5:6, 0:points] == wanted), 1.0, 0.0)
                chosen = chosen.astype(jnp.bfloat16)
                parts = []
                for table in (s_xi * l_eta, l_xi * s_eta, factor * (l_xi * l_eta)):
                    high, low = halves(table)
                    parts.append(dot(chosen, high) + dot(chosen, low))
                return jnp.concatenate(parts, axis=0)

            @pl.loop(0, n // 2)
            def _(j):
                first, second = block_mix(2 * j), pltpu.roll(block_mix(2 * j + 1), slot, 1)
                mix[j] = mix[j] + first + jnp.where(upper, second, 0.0)
                mix[j + 1] = mix[j + 1] + jnp.where(upper, 0.0, second)

        pl.when(has_left)(lambda: left_force(step).wait_send())
        pl.when(has_right)(lambda: right_force(step).wait_send())
        pl.when(has_right)(lambda: left_force(step).wait_recv())
        pl.when(has_left)(lambda: right_force(step).wait_recv())
        from_left = fl_in[step]
        for a in range(nr):
            ahead[a] = ahead[a] + jnp.where(
                (row == 0)[None], inv_main[a] * from_left[:, a : a + 1, :], 0.0
            )
        rim_ahead = 2.0 * rim - rim_before + inv_rim * (rim_force + fr_in[step])
        rim_ahead = jnp.where(has_right, rim_ahead, 0.0)
        before, u, rim_before, rim = u, ahead, rim, rim_ahead

    for a in range(nr):
        gathered[o, :, a * cols : (a + 1) * cols, :] = u[a]
    lo, hi, groups = lax.rem(o, 2), lax.div(o, 2), n // 2
    partner = hi * 2 + 1 - lo

    def far(h):
        block = gathered.at[o, :, 0:nodes, :]
        to = lax.rem(hi + h, groups) * 2 + lo
        return remote(block, block, ga_s.at[h], ga_r.at[h], (to, q))

    def near(h):
        block = gathered.at[lax.rem(hi + groups - h, groups) * 2 + lo, :, 0:nodes, :]
        return remote(block, block, gb_s.at[h], gb_r.at[h], (partner, q))

    pl.loop(1, groups)(lambda h: far(h).start())
    near(0).start()
    for a in range(nr):
        out_u[:, a] = u[a]
    for copy in basis_copies:
        copy.wait()

    @pl.loop(1, groups)
    def _(h):
        far(h).wait_recv()
        near(h).start()

    for h in range(1, az):
        adj_copy(h).wait_send()
        adj_copy(h).wait_recv()
    pl.loop(0, groups)(lambda h: near(h).wait_recv())

    def block_of(j, s):
        return jnp.concatenate([gathered[2 * j, s], gathered[2 * j + 1, s]], axis=0)

    def add_pair(j, total):
        left = halves(mix[j])
        return tuple(total[s] + dot3(left, halves(block_of(j, s))) for s in range(comps))

    zero = jnp.zeros((3 * cells, width), jnp.float32)
    coefs = lax.fori_loop(0, groups, add_pair, (zero,) * comps)
    rows = []
    for s in range(comps):
        rows.append(coefs[s][0 : 2 * cells])
        rows.append(swap(coefs[s][2 * cells :]) * ratio)
    split = halves(jnp.concatenate(rows, axis=0))
    raw = []
    for h in range(az):
        r = lax.rem(q + h, az)
        samples = dot3(split, (bh[r], bl[r]))
        total = jnp.zeros((cells, width), jnp.float32)
        for g in range(3 * comps):
            values = adjoint[g] if h == 0 else adj_all[h, g]
            total = total + samples[g * cells : (g + 1) * cells] * values
        raw.append(total)
    raw = jnp.concatenate(raw, axis=1)
    whole = az * width
    for h in range(az):
        at = slice(h * width, (h + 1) * width)
        face_out[0, h] = raw[0:depth, at]
        face_out[1, h] = raw[cells - depth :, at]

    def face_left(h):
        return remote(
            face_out.at[0, h], face_in.at[1, h], face_s.at[0, h], face_r.at[0, h],
            (o - 1, lax.rem(q + h, az)),
        )

    def face_right(h):
        return remote(
            face_out.at[1, h], face_in.at[0, h], face_s.at[1, h], face_r.at[1, h],
            (o + 1, lax.rem(q + h, az)),
        )

    for h in range(az):
        pl.when(has_left)(lambda: face_left(h).start())
        pl.when(has_right)(lambda: face_right(h).start())
    level = lax.broadcasted_iota(jnp.int32, (cells, whole), 0)
    level_in = level % depth
    around = pltpu.roll(raw, 1, 1) + pltpu.roll(raw, whole - 1, 1)
    around = around + jnp.where(level_in > 0, pltpu.roll(raw, 1, 0), 0.0)
    around = around + jnp.where(level_in < depth - 1, pltpu.roll(raw, cells - 1, 0), 0.0)
    around = around + jnp.where(level >= depth, pltpu.roll(raw, depth, 0), 0.0)
    around = around + jnp.where(level < cells - depth, pltpu.roll(raw, cells - depth, 0), 0.0)
    smooth = (1.0 - 6.0 * smooth_rate) * raw + smooth_rate * around

    def part_copy(h):
        return remote(
            part_out.at[h], part_in.at[h], part_s.at[h], part_r.at[h], (o, lax.rem(q + h, az))
        )

    for h in range(1, az):
        part_out[h] = smooth[:, h * width : (h + 1) * width]
        part_copy(h).start()
    result = smooth[:, 0:width]
    for h in range(1, az):
        part_copy(h).wait_recv()
        result = result + part_in[h]
    for h in range(az):
        pl.when(has_right)(lambda: face_left(h).wait_recv())
        pl.when(has_left)(lambda: face_right(h).wait_recv())
    below, above = face_in[0, 0], face_in[1, 0]
    for h in range(1, az):
        below, above = below + face_in[0, h], above + face_in[1, h]
    out_k[...] = result
    out_k[0:depth] = result[0:depth] + smooth_rate * below
    out_k[cells - depth :] = out_k[cells - depth :] + smooth_rate * above

    for h in range(1, az):
        part_copy(h).wait_send()
    for h in range(az):
        pl.when(has_left)(lambda: face_left(h).wait_send())
        pl.when(has_right)(lambda: face_right(h).wait_send())
    pl.loop(1, groups)(lambda h: far(h).wait_send())
    pl.loop(0, groups)(lambda h: near(h).wait_send())


def on_device(
    n, az, disp, vel, modulus, hoop, coupling, density, orders, element, local, scale, owner, cell,
    adjoint,
):
    comps, nr, cols, width = disp.shape
    elements, points = modulus.shape[1], owner.shape[0]
    layers, lats, phi_width = adjoint.shape[1:]
    cells = layers * lats
    turned = jnp.swapaxes(adjoint, 1, 2).reshape(9, cells, phi_width)
    high, low = basis_tables(az, width, phi_width)
    vm, sm = pl.BlockSpec(memory_space=pltpu.VMEM), pl.BlockSpec(memory_space=pltpu.SMEM)
    anywhere = pl.BlockSpec(memory_space=pl.ANY)
    slot = width // 2
    f32, dma = jnp.float32, pltpu.SemaphoreType.DMA
    buf = lambda *shape: pltpu.VMEM(shape, f32)
    final, smoothed = pl.pallas_call(
        functools.partial(kernel, n, az),
        out_shape=(
            jax.ShapeDtypeStruct(disp.shape, f32),
            jax.ShapeDtypeStruct((cells, phi_width), f32),
        ),
        in_specs=[vm, vm, sm, sm, sm, sm, sm] + [vm] * 6 + [anywhere] * 2 + [vm] * 3,
        out_specs=(vm, vm),
        scratch_shapes=[
            buf(2 * comps + 1, cols, width), buf(2 * comps + 1, cols, width),
            buf(cols, width), buf(cols, width),
            buf(STEPS, comps, cols, width), buf(STEPS, comps, cols, width),
            buf(STEPS, comps, cols, width), buf(STEPS, comps, cols, width),
            buf(n, 8, width), buf(n, comps, slot, width), buf(n // 2 + 1, 3 * cells, width),
            buf(az, 9, cells, phi_width),
            pltpu.VMEM((az, width, phi_width), jnp.bfloat16),
            pltpu.VMEM((az, width, phi_width), jnp.bfloat16),
            buf(az, cells, phi_width), buf(az, cells, phi_width),
            buf(2, az, layers, phi_width), buf(2, az, layers, phi_width),
            dma, dma, dma, dma, dma((2, STEPS)), dma((2, STEPS)), dma((n,)), dma((n,)),
            dma((az,)), dma((az,)), dma((n,)), dma((n,)), dma((n,)), dma((n,)),
            dma((az,)), dma((az,)), dma((2, az)), dma((2, az)), dma((2,)),
        ],
        compiler_params=pltpu.CompilerParams(
            collective_id=0, has_side_effects=True, vmem_limit_bytes=40 * 1024 * 1024
        ),
    )(
        disp, vel, modulus, hoop, coupling, density, orders, element, local,
        scale.reshape(1, points), owner, cell.reshape(1, points), turned,
        jnp.asarray(high), jnp.asarray(low),
        jnp.asarray(lane_table(elements, cols, width)),
        jnp.asarray(column_table(elements, cols, width)),
        jnp.asarray(rim_table(cols, width)),
    )
    return final, jnp.swapaxes(smoothed.reshape(lats, layers, phi_width), 0, 1)


def solution(mesh):
    field = P(None, None, "mer", "az")
    placed = (
        field, field, P(None, "mer"), P(None, "mer"), P(None, "mer"), P(None, "mer"),
        P(None, "mer"), P("mer", None), P("mer", None), P("mer"), P("mer", None), P("mer"), field,
    )
    return jax.shard_map(
        functools.partial(on_device, mesh.shape["mer"], mesh.shape["az"]),
        mesh=mesh,
        in_specs=placed,
        out_specs=(field, P(None, "mer", "az")),
        check_vma=False,
    )
```

time: 188 us -> 42.4 us (0.23)
  waiting for transfers between devices: 54.8 us -> 0 us
  starting transfers between devices: 45 us -> 0 us
  Pallas kernels: 0 us -> 34.2 us
  other arithmetic: 22.6 us -> 0 us
  local copies, waits for them, and re-layouts: 28.5 us -> 7.06 us
  matrix products: 21.3 us -> 0 us
  between operations: 15.5 us -> 0.81 us
    pallas_call x0 -> x1, Pallas kernels: none -> 34.2 us  [on_device(): pl.pallas_call(functools.partial(kernel, n, az), out_shape=(jax.ShapeDtyp...]
    ppermute x12 -> x0, starting transfers between devices: 29.5 us -> none  [the longest x8 23 us: from_behind(): lax.ppermute(value, axis, [(source, source + steps) for source in range(f...]
    dot_general x19 -> x0, matrix products: 21.3 us -> none  [the longest x1 4.45 us: point_gradients(): jnp.einsum('pa,pb,cpabk->pck', xi_values, eta_values, gathered, precision...]
    reduce_scatter x1 -> x0, waiting for transfers between devices: 21.1 us -> none  [on_device(): lax.psum_scatter(jnp.einsum('kj,cgk->jgc', basis, voxel_coefs, precision=...]
    all_to_all x2 -> x0, waiting for transfers between devices: 17.5 us -> none  [the longest x1 17.5 us: on_device(): lax.all_to_all(outgoing, 'mer', split_axis=0, concat_axis=0, tiled=True)]
    ppermute x12 -> x0, waiting for transfers between devices: 16.2 us -> none  [the longest x8 13.7 us: from_behind(): lax.ppermute(value, axis, [(source, source + steps) for source in range(f...]
    all_to_all x2 -> x0, starting transfers between devices: 15.3 us -> none  [the longest x1 8.01 us: on_device(): lax.all_to_all(outgoing, 'mer', split_axis=0, concat_axis=0, tiled=True)]
    scatter-add x26 -> x0, other arithmetic: 12.9 us -> none  [the longest x20 12.9 us: from_elements(): assembled.at[:, :, b:b + 4 * count_cols:4].add(radial[:, :, :, b])]
  transfers between devices with their start and end apart: 15 -> 0, of which waited for: 11 -> 0; matrix products, arithmetic and copies ran while one was open for 34% -> 0% of each run, Pallas kernels for 0% -> 0%
where the time goes in v1:
time: 42.4 us; the launch traced here: 42.1 us
  Pallas kernels  34.2 us (81%)
  local copies, waits for them, and re-layouts  7.06 us (17%)
  between operations  0.81 us (2%)
    pallas_call x1, Pallas kernels, on_device(): pl.pallas_call(functools.partial(kernel, n, az), out_shape=(jax.ShapeDtyp...  34.2 us
    unnamed x38, local copies, waits for them, and re-layouts  5.43 us
    transpose x1, local copies, waits for them, and re-layouts, on_device(): turned = jnp.swapaxes(adjoint, 1, 2).reshape(9, cells, phi_width)  1.02 us

profile of v1, /device:TPU:0, one launch (start us, length us, event | category | flops | bytes accessed | tf_op | source)
XLA Modules:
  0.0 42.1 jit_solution(4355377091933384142)
XLA Ops:
  0.6 0.7 %copy-done.14 = s32[64,2]{0,1:T(2,128)S(1)} copy-done((s32[64,2]{0,1:T(2,128)S(1)}, s32[64,2]{0,1:T(2,128)}, u32[]{:S(2)}) %copy-start.14) | copy-done | bytes 536
  1.3 0.1 copy.21.element
  1.4 0.6 %copy-done.15 = f32[64,2]{0,1:T(2,128)S(1)} copy-done((f32[64,2]{0,1:T(2,128)S(1)}, f32[64,2]{0,1:T(2,128)}, u32[]{:S(2)}) %copy-start.15) | copy-done | bytes 536
  2.0 0.1 copy.22.local
  2.1 0.6 %copy-done.16 = s32[64,1]{0,1:T(1,128)S(1)} copy-done((s32[64,1]{0,1:T(1,128)S(1)}, s32[64,1]{0,1:T(1,128)}, u32[]{:S(2)}) %copy-start.16) | copy-done | bytes 280
  2.6 0.1 copy.23.owner
  2.8 0.0 copy-start.4
  2.8 0.0 copy-start.5
  2.8 0.0 copy-start.6
  2.8 0.0 copy-start.10
  2.8 0.0 copy-start.11
  2.8 0.0 copy-start.12
  2.8 0.0 copy-start.13
  2.8 1.0 %copy.27 = f32[9,4,8,128]{3,2,1,0:T(8,128)S(1)} copy(f32[9,4,8,128]{3,1,2,0:T(4,128)} %bitcast.14) | data formatting | bytes 294912 | tf_op jit(solution)/shard_map/transpose | solution.py:495
  3.9 0.0 copy-start.7
  3.9 0.0 copy-start.8
  4.0 0.5 %copy-done.7 = f32[1,2]{1,0:T(1,128)S(1)} copy-done((f32[1,2]{1,0:T(1,128)S(1)}, f32[1,2]{1,0:T(1,128)}, u32[]{:S(2)}) %copy-start.7) | copy-done | bytes 32
  4.5 0.0 copy-done.8
  4.5 0.0 copy-done.9
  4.5 1.0 %copy-done = bf16[4,4,128,128]{3,2,1,0:T(8,128)(2,1)S(1)} copy-done((bf16[4,4,128,128]{3,2,1,0:T(8,128)(2,1)S(1)}, bf16[4,4,128,128]{3,2,1,0:T(8,128)(2,1)}, u32[]{:S(2)}) %copy-start) | copy-done | bytes 524312
  5.6 1.0 %copy-done.1 = bf16[4,4,128,128]{3,2,1,0:T(8,128)(2,1)S(1)} copy-done((bf16[4,4,128,128]{3,2,1,0:T(8,128)(2,1)S(1)}, bf16[4,4,128,128]{3,2,1,0:T(8,128)(2,1)}, u32[]{:S(2)}) %copy-start.1) | copy-done | bytes 524312
  6.6 34.2 %shard_map.185 = (f32[3,5,8,128]{3,2,1,0:T(8,128)S(1)}, f32[32,128]{1,0:T(8,128)S(1)}) custom-call(f32[3,5,8,128]{3,2,1,0:T(8,128)S(1)} %copy-done.3, f32[3,5,8,128]{3,2,1,0:T(8,128)S(1)} %copy-done.4, f32[1,2]{1,0:T(1,128)S(1)} %copy-done.7, f32[1,2]{1,0:T(1,128)S(1)} %copy-done.8, f32[1,2]{1,0:T(1,128)S(1)} %copy-done.9, f32[1,2]{1,0:T(1,128)S(1)} %copy-done.10, ...), custom_call_target="tpu_custom_call" | custom-call | tf_op jit(solution)/shard_map/pallas_call | solution.py:502
  40.9 0.6 %copy.28 = f32[4,8,128]{2,0,1:T(4,128)} copy(f32[4,8,128]{2,1,0:T(8,128)S(1)} %bitcast.11) | data formatting | bytes 32768 | tf_op jit(solution)/shard_map/reshape | solution.py:536
  41.5 0.6 %copy.30 = f32[3,5,8,128]{3,2,1,0:T(8,128)} copy(f32[3,5,8,128]{3,2,1,0:T(8,128)S(1)} %get-tuple-element.8) | data formatting | bytes 122880
  (17 shorter events, 0.0 us)
Async XLA Ops:
  0.6 0.7 %copy-start.14 = (s32[64,2]{0,1:T(2,128)S(1)}, s32[64,2]{0,1:T(2,128)}, u32[]{:S(2)}) copy-start(s32[64,2]{0,1:T(2,128)} %param.25) | copy-start | bytes 1540
  1.3 0.7 %copy-start.15 = (f32[64,2]{0,1:T(2,128)S(1)}, f32[64,2]{0,1:T(2,128)}, u32[]{:S(2)}) copy-start(f32[64,2]{0,1:T(2,128)} %param.26) | copy-start | bytes 1540
  2.0 0.7 %copy-start.16 = (s32[64,1]{0,1:T(1,128)S(1)}, s32[64,1]{0,1:T(1,128)}, u32[]{:S(2)}) copy-start(s32[64,1]{0,1:T(1,128)} %param.28) | copy-start | bytes 772
  2.7 1.2 %copy-start.2 = (f32[2,10,8,128]{3,2,1,0:T(8,128)S(1)}, f32[2,10,8,128]{3,2,1,0:T(8,128)}, u32[]{:S(2)}) copy-start(f32[2,10,8,128]{3,2,1,0:T(8,128)} %constant.13.clone.cols_t) | copy-start | bytes 245764
  2.7 1.2 %copy-start.3 = (f32[3,5,8,128]{3,2,1,0:T(8,128)S(1)}, f32[3,5,8,128]{3,2,1,0:T(8,128)}, u32[]{:S(2)}) copy-start(f32[3,5,8,128]{3,2,1,0:T(8,128)} %disp.1) | copy-start | bytes 184324
  2.8 1.2 %copy-start.4 = (f32[3,5,8,128]{3,2,1,0:T(8,128)S(1)}, f32[3,5,8,128]{3,2,1,0:T(8,128)}, u32[]{:S(2)}) copy-start(f32[3,5,8,128]{3,2,1,0:T(8,128)} %vel.1) | copy-start | bytes 184324
  2.8 1.2 %copy-start.5 = (f32[8,8,128]{2,1,0:T(8,128)S(1)}, f32[8,8,128]{2,1,0:T(8,128)}, u32[]{:S(2)}) copy-start(f32[8,8,128]{2,1,0:T(8,128)} %constant.14.clone.rim_t) | copy-start | bytes 98308
  2.8 1.2 %copy-start.6 = (f32[27,128]{1,0:T(8,128)S(1)}, f32[27,128]{1,0:T(8,128)}, u32[]{:S(2)}) copy-start(f32[27,128]{1,0:T(8,128)} %constant.12.clone.lanes_t) | copy-start | bytes 41476
  2.8 1.2 %copy-start.10 = (f32[1,2]{1,0:T(1,128)S(1)}, f32[1,2]{1,0:T(1,128)}, u32[]{:S(2)}) copy-start(f32[1,2]{1,0:T(1,128)} %density.1) | copy-start | bytes 28
  2.8 1.2 %copy-start.11 = (s32[1,2]{1,0:T(1,128)S(1)}, s32[1,2]{1,0:T(1,128)}, u32[]{:S(2)}) copy-start(s32[1,2]{1,0:T(1,128)} %orders.1) | copy-start | bytes 28
  2.8 1.2 %copy-start.12 = (f32[64]{0:T(128)S(1)}, f32[64]{0:T(128)}, u32[]{:S(2)}) copy-start(f32[64]{0:T(128)} %param.27) | copy-start | bytes 772
  2.8 1.1 %copy-start.13 = (s32[64]{0:T(128)S(1)}, s32[64]{0:T(128)}, u32[]{:S(2)}) copy-start(s32[64]{0:T(128)} %param.29) | copy-start | bytes 772
  3.9 0.7 %copy-start.7 = (f32[1,2]{1,0:T(1,128)S(1)}, f32[1,2]{1,0:T(1,128)}, u32[]{:S(2)}) copy-start(f32[1,2]{1,0:T(1,128)} %modulus.1) | copy-start | bytes 28
  3.9 0.7 %copy-start.8 = (f32[1,2]{1,0:T(1,128)S(1)}, f32[1,2]{1,0:T(1,128)}, u32[]{:S(2)}) copy-start(f32[1,2]{1,0:T(1,128)} %hoop.1) | copy-start | bytes 28
  3.9 0.7 %copy-start.9 = (f32[1,2]{1,0:T(1,128)S(1)}, f32[1,2]{1,0:T(1,128)}, u32[]{:S(2)}) copy-start(f32[1,2]{1,0:T(1,128)} %coupling.1) | copy-start | bytes 28
  4.5 1.0 %copy-start = (bf16[4,4,128,128]{3,2,1,0:T(8,128)(2,1)S(1)}, bf16[4,4,128,128]{3,2,1,0:T(8,128)(2,1)}, u32[]{:S(2)}) copy-start(bf16[4,4,128,128]{3,2,1,0:T(8,128)(2,1)} %constant.11.clone.blo) | copy-start | bytes 1572868
  5.6 1.0 %copy-start.1 = (bf16[4,4,128,128]{3,2,1,0:T(8,128)(2,1)S(1)}, bf16[4,4,128,128]{3,2,1,0:T(8,128)(2,1)}, u32[]{:S(2)}) copy-start(bf16[4,4,128,128]{3,2,1,0:T(8,128)(2,1)} %constant.10.clone.bhi) | copy-start | bytes 1572868

commit v2 on v1

--- a/solution.py
+++ b/solution.py
@@ -35,22 +35,16 @@
     return weights, monomials, slopes, stiffness
 
 
-def lane_table(elements, cols, lanes):
+def point_table(elements, cols, lanes):
     _, monomials, slopes, _ = gll_tables()
-    table = np.zeros((9 * (1 + elements), lanes), np.float32)
-    for lane in range(lanes):
-        half, spot = divmod(lane, lanes // 2)
-        a, col = divmod(spot, cols)
-        if a > 4 or (half and col):
-            continue
-        col = cols if half else col
-        table[0:5, lane], table[5:9, lane] = monomials[a], slopes[a]
-        for e in range(elements):
-            b = col - 4 * e
-            if 0 <= b <= 4:
-                at = 9 * (1 + e)
-                table[at : at + 5, lane], table[at + 5 : at + 9, lane] = monomials[b], slopes[b]
-    return table
+    both = np.concatenate([monomials, slopes], axis=1)
+    table = np.zeros((1 + elements, 9, cols, lanes), np.float32)
+    table[0, :, 0:5] = both.T[:, :, None]
+    for e in range(elements):
+        for c in range(cols):
+            if 0 <= c - 4 * e <= 4:
+                table[1 + e, :, c] = both[c - 4 * e][:, None]
+    return table.reshape(-1, cols, lanes)
 
 
 def column_table(elements, cols, lanes):
@@ -87,11 +81,15 @@
     k, j = np.arange(coefs)[:, None], np.arange(phis)[None, :]
     angles = (k // 2) * j % (2 * ORDERS) * (2.0 * math.pi / (2 * ORDERS))
     basis = np.where(k % 2 == 0, np.cos(angles), np.sin(angles)) / math.sqrt(ORDERS)
-    basis = basis.reshape(az_count, width, az_count, phi_width).transpose(0, 2, 1, 3)
-    basis = basis.astype(np.float32)
+    basis = basis.reshape(az_count, width, az_count, phi_width)
+    turned = [
+        np.concatenate([basis[q, :, (q + h) % az_count] for h in range(az_count)], axis=1)
+        for q in range(az_count)
+    ]
+    basis = np.stack(turned).astype(np.float32)
     high = basis.astype(ml_dtypes.bfloat16)
     low = (basis - high.astype(np.float32)).astype(ml_dtypes.bfloat16)
-    return high, low
+    return np.concatenate([high, high, low], axis=1)
 
 
 def halves(x):
@@ -103,29 +101,46 @@
     return jnp.dot(x, y, preferred_element_type=jnp.float32)
 
 
-def dot3(x, y):
-    (xh, xl), (yh, yl) = x, y
-    return dot(xh, yh) + (dot(xl, yh) + dot(xh, yl))
+def left_parts(x):
+    high, low = halves(x)
+    return jnp.concatenate([high, low, high], axis=1)
+
+
+def right_parts(x):
+    high, low = halves(x)
+    return jnp.concatenate([high, high, low], axis=0)
 
 
 def kernel(
-    n, az, disp, vel, modulus, hoop, coupling, density, orders, element, local, scale, owner, cell,
-    adjoint, bhi, blo, lanes_t, cols_t, rim_t, out_u, out_k,
+    n, az, disp_a, vel_a, modulus_a, hoop_a, coupling_a, density_a, orders_a, element_a, local_a,
+    scale_a, owner_a, cell_a, adjoint_a, basis_a, tiles_a, out_u, out_k,
+    disp, vel, modulus, hoop, coupling, density, orders, element, local, scale, owner, cell,
+    adjoint, basis, tiles, final,
     halo_out, halo_in, dens_out, dens_in, fl_out, fr_out, fl_in, fr_in, meta, gathered, mix,
-    adj_all, bh, bl, part_out, part_in, face_out, face_in,
+    adj_all, part_out, part_in, face_out, face_in,
     halo_s, halo_r, dens_s, dens_r, f_s, f_r, meta_s, meta_r, adj_s, adj_r, ga_s, ga_r, gb_s, gb_r,
-    part_s, part_r, face_s, face_r, b_s,
+    part_s, part_r, face_s, face_r, in_s, out_s,
 ):
     o, q = lax.axis_index("mer"), lax.axis_index("az")
     comps, nr, cols, width = disp.shape
     elements = modulus.shape[1]
-    points = owner.shape[0]
+    points = owner.shape[1]
     slot = gathered.shape[2]
     nodes = nr * cols
     cells = adjoint.shape[1]
     depth = face_in.shape[2]
+    lats = cells // depth
     weights, _, _, stiffness = gll_tables()
     has_left, has_right = o > 0, o < n - 1
+    pairs = [
+        (disp_a, disp), (vel_a, vel), (modulus_a, modulus), (hoop_a, hoop), (coupling_a, coupling),
+        (density_a, density), (orders_a, orders), (element_a, element), (local_a, local),
+        (scale_a, scale), (owner_a, owner), (cell_a, cell), (tiles_a, tiles), (adjoint_a, adjoint),
+        (basis_a.at[q], basis),
+    ]
+    fetches = [pltpu.make_async_copy(src, dst, in_s.at[i]) for i, (src, dst) in enumerate(pairs)]
+    for fetch in fetches:
+        fetch.start()
 
     halo_in[...] = jnp.zeros_like(halo_in)
     dens_in[...] = jnp.zeros_like(dens_in)
@@ -152,12 +167,8 @@
         def _():
             pl.semaphore_signal(barrier, inc=1, device_id=(o + 1, r), device_id_type=MESH)
 
-    basis_copies = [
-        pltpu.make_async_copy(bhi.at[q], bh, b_s.at[0]),
-        pltpu.make_async_copy(blo.at[q], bl, b_s.at[1]),
-    ]
-    for copy in basis_copies:
-        copy.start()
+    for fetch in fetches[:-2]:
+        fetch.wait()
 
     row = lax.broadcasted_iota(jnp.int32, (cols, width), 0)
     lane = lax.broadcasted_iota(jnp.int32, (1, width), 1)
@@ -172,18 +183,10 @@
 
     halo_out[0:comps] = first_column(u)
     halo_out[comps : 2 * comps] = first_column(v)
-    halo_out[2 * comps] = jnp.full((cols, width), density[0, 0])
-    dens_out[...] = jnp.full((cols, width), density[0, elements - 1])
-    eye = lax.broadcasted_iota(jnp.int32, (points, width), 0) == lax.broadcasted_iota(
-        jnp.int32, (points, width), 1
-    )
-
-    def as_row(column):
-        return jnp.sum(jnp.where(eye, column, 0.0), axis=0, keepdims=True)
-
-    def as_column(line):
-        return jnp.sum(jnp.where(eye, line, 0.0), axis=1, keepdims=True)
-
+    halo_out[2 * comps] = jnp.broadcast_to(density[0:1, 0:1], (cols, width))
+    dens_out[...] = jnp.broadcast_to(
+        density[0:1, elements - 1 : elements], (cols, width)
+    )
     spare = jnp.zeros((1, width - points), jnp.float32) if width > points else None
 
     def wide(line):
@@ -191,10 +194,10 @@
 
     meta[o] = jnp.concatenate(
         [
-            as_row(local[:, 0:1]),
-            as_row(local[:, 1:2]),
-            as_row((element[:, 1:2] % elements).astype(jnp.float32)),
-            as_row(owner[:, 0:1].astype(jnp.float32)),
+            wide(local[0:1, :]),
+            wide(local[1:2, :]),
+            wide((element[1:2, :] % elements).astype(jnp.float32)),
+            wide(owner[...].astype(jnp.float32)),
             wide(scale[...]),
             wide(cell[...].astype(jnp.float32)),
             jnp.zeros((2, width), jnp.float32),
@@ -228,46 +231,50 @@
             adjoint, adj_all.at[h], adj_s.at[h], adj_r.at[h], (o, lax.rem(q + az - h, az))
         )
 
+    fetches[-2].wait()
     for h in range(1, az):
         adj_copy(h).start()
 
     order = (q * width + lane) // 2
     ratio = order.astype(jnp.float32) / ORDERS
     even = (lane % 2 == 0)
-    keep = [jnp.where(order < orders[0, e], 1.0, 0.0) for e in range(elements)]
-    mod = [modulus[0, e] * keep[e] for e in range(elements)]
-    hp = [hoop[0, e] * keep[e] * (ratio * ratio) for e in range(elements)]
-    cp = [coupling[0, e] * keep[e] * ratio for e in range(elements)]
+    one = lambda ref, e: ref[0:1, e : e + 1]
+    keep = [jnp.where(order < one(orders, e), 1.0, 0.0) for e in range(elements)]
+    mod = [one(modulus, e) * keep[e] for e in range(elements)]
+    hp = [one(hoop, e) * keep[e] * (ratio * ratio) for e in range(elements)]
+    cp = [one(coupling, e) * keep[e] * ratio for e in range(elements)]
+    points_at = 0
+    cols_at = 9 * (1 + elements)
+    rim_at = cols_at + elements * (cols + 2)
+    cols_t = lambda e, which: tiles[cols_at + e * (cols + 2) + which]
     last = elements - 1
     w_end = float(weights[4])
 
     def blend(per_element, which):
-        total = per_element[0] * cols_t[0, which]
+        total = per_element[0] * cols_t(0, which)
         for e in range(1, elements):
-            total = total + per_element[e] * cols_t[e, which]
+            total = total + per_element[e] * cols_t(e, which)
         return total
 
     c_radial, c_hoop, c_pair = blend(mod, 0), blend(hp, 0), blend(cp, 0)
     c_colat = [blend(mod, 1 + d) for d in range(cols)]
-    c_rim = mod[last] * cols_t[last, cols + 1]
+    c_rim = mod[last] * cols_t(last, cols + 1)
     w_rim = jnp.zeros((cols, width), jnp.float32)
     for a in range(nr):
         w_rim = jnp.where(row == a, float(weights[a]), w_rim)
-    r_radial = [mod[last] * w_end * rim_t[d] for d in range(cols)]
+    r_radial = [mod[last] * w_end * tiles[rim_at + d] for d in range(cols)]
     r_radial[0] = r_radial[0] + w_rim * (
         mod[last] * float(stiffness[4, 4]) + hp[last] * w_end
     )
     r_pair = w_rim * (cp[last] * w_end)
 
-    pl.when(has_left)(lambda: to_left().wait_send())
-    pl.when(has_right)(lambda: to_right().wait_send())
     pl.when(has_right)(lambda: to_left().wait_recv())
     pl.when(has_left)(lambda: to_right().wait_recv())
-    col_mass = density[0, 0] * cols_t[0, 0]
+    col_mass = one(density, 0) * cols_t(0, 0)
     for e in range(1, elements):
-        col_mass = col_mass + density[0, e] * cols_t[e, 0]
+        col_mass = col_mass + one(density, e) * cols_t(e, 0)
     col_mass = col_mass + jnp.where(row == 0, w_end * dens_in[...], 0.0)
-    rim_mass = w_end * (density[0, last] + halo_in[2 * comps])
+    rim_mass = w_end * (one(density, last) + halo_in[2 * comps])
     inv_main = [step_scale / (float(weights[a]) * col_mass) for a in range(nr)]
     inv_rim = step_scale / (jnp.where(row < nr, w_rim, 1.0) * rim_mass)
     inv_rim = jnp.where(has_right, inv_rim, 0.0)
@@ -290,6 +297,58 @@
 
     def right_force(step):
         return remote(fr_out.at[step], fl_in.at[step], f_s.at[1, step], f_r.at[1, step], (o + 1, q))
+
+    wanted = lax.broadcasted_iota(jnp.int32, (cells, width), 0).astype(jnp.float32)
+    upper = lane >= slot
+    blank = jnp.zeros((slot - nodes, width), jnp.float32)
+    _, monomials, slopes, _ = gll_tables()
+
+    def horner(x, coefs):
+        total = coefs[-1]
+        for coef in coefs[-2::-1]:
+            total = total * x + coef
+        return total
+
+    def tile_horner(x, at, count):
+        return horner(x, [tiles[points_at + at + p] for p in range(count)])
+
+    def block_mix(i):
+        line = lambda k: meta[i, k : k + 1, :]
+        xi, eta, spot, factor = line(0), line(1), line(2), line(4)
+        l_xi, s_xi = tile_horner(xi, 0, 5), tile_horner(xi, 5, 4)
+        l_eta, s_eta = tile_horner(eta, 9, 5), tile_horner(eta, 14, 4)
+        for e in range(1, elements):
+            here = spot == float(e)
+            l_eta = jnp.where(here, tile_horner(eta, 9 + 9 * e, 5), l_eta)
+            s_eta = jnp.where(here, tile_horner(eta, 14 + 9 * e, 4), s_eta)
+        at_end = spot == float(elements - 1)
+        l_end = jnp.where(at_end, horner(eta, [float(x) for x in monomials[4]]), 0.0)
+        s_end = jnp.where(at_end, horner(eta, [float(x) for x in slopes[4]]), 0.0)
+        parts = []
+        for x, y, y_end in (
+            (s_xi, l_eta, l_end), (l_xi, s_eta, s_end), (factor * l_xi, l_eta, l_end)
+        ):
+            parts += [x[a : a + 1, :] * y for a in range(nr)] + [blank]
+            end = x * y_end
+            parts += [jnp.where(row == 0, end[a : a + 1, :], 0.0) for a in range(nr)] + [blank]
+        high, low = halves(jnp.concatenate(parts, axis=0))
+        chosen = (line(3) == o.astype(jnp.float32)) & (line(5) == wanted)
+        chosen = chosen & (lane < points)
+        chosen = jnp.where(chosen, 1.0, 0.0).astype(jnp.bfloat16)
+        taken = lax.dot_general(
+            jnp.concatenate([chosen, chosen], axis=1),
+            jnp.concatenate([high, low], axis=1),
+            (((1,), (1,)), ((), ())),
+            preferred_element_type=jnp.float32,
+        )
+        return jnp.concatenate([taken[:, t * width : (t + 1) * width] for t in range(3)], axis=0)
+
+    def mix_blocks(start, stop):
+        @pl.loop(start, stop)
+        def _(j):
+            first, second = block_mix(2 * j), pltpu.roll(block_mix(2 * j + 1), slot, 1)
+            mix[j] = mix[j] + first + jnp.where(upper, second, 0.0)
+            mix[j + 1] = mix[j + 1] + jnp.where(upper, 0.0, second)
 
     for step in range(STEPS):
         forces, rim_force = [], jnp.zeros((comps, cols, width), jnp.float32)
@@ -316,47 +375,9 @@
         pl.when(has_right)(lambda: right_force(step).start())
         ahead = [2.0 * u[a] - before[a] + inv_main[a] * forces[a] for a in range(nr)]
         if step == 0:
-            pl.loop(1, n)(lambda h: meta_copy(h).wait_send())
             pl.loop(1, n)(lambda h: meta_copy(h).wait_recv())
             mix[...] = jnp.zeros_like(mix)
-            wanted = lax.broadcasted_iota(jnp.int32, (cells, points), 0)
-            wanted = ((wanted % depth) * (cells // depth) + wanted // depth).astype(jnp.float32)
-            upper = lane >= slot
-
-            def horner(x, at, count):
-                total = lanes_t[at + count - 1 : at + count, :]
-                for p in range(count - 2, -1, -1):
-                    total = total * x + lanes_t[at + p : at + p + 1, :]
-                return total
-
-            def block_mix(i):
-                xi, eta = as_column(meta[i, 0:1, :]), as_column(meta[i, 1:2, :])
-                spot, factor = as_column(meta[i, 2:3, :]), as_column(meta[i, 4:5, :])
-                xi = jnp.broadcast_to(xi, (points, width))
-                eta = jnp.broadcast_to(eta, (points, width))
-                l_xi, s_xi = horner(xi, 0, 5), horner(xi, 5, 4)
-                l_eta, s_eta = horner(eta, 9, 5), horner(eta, 14, 4)
-                for e in range(1, elements):
-                    here = spot == float(e)
-                    l_eta = jnp.where(here, horner(eta, 9 + 9 * e, 5), l_eta)
-                    s_eta = jnp.where(here, horner(eta, 14 + 9 * e, 4), s_eta)
-                mine = meta[i, 3:4, 0:points] == o.astype(jnp.float32)
-                chosen = jnp.where(mine & (meta[i, 5:6, 0:points] == wanted), 1.0, 0.0)
-                chosen = chosen.astype(jnp.bfloat16)
-                parts = []
-                for table in (s_xi * l_eta, l_xi * s_eta, factor * (l_xi * l_eta)):
-                    high, low = halves(table)
-                    parts.append(dot(chosen, high) + dot(chosen, low))
-                return jnp.concatenate(parts, axis=0)
-
-            @pl.loop(0, n // 2)
-            def _(j):
-                first, second = block_mix(2 * j), pltpu.roll(block_mix(2 * j + 1), slot, 1)
-                mix[j] = mix[j] + first + jnp.where(upper, second, 0.0)
-                mix[j + 1] = mix[j + 1] + jnp.where(upper, 0.0, second)
-
-        pl.when(has_left)(lambda: left_force(step).wait_send())
-        pl.when(has_right)(lambda: right_force(step).wait_send())
+        mix_blocks(n // 2 * step // STEPS, n // 2 * (step + 1) // STEPS)
         pl.when(has_right)(lambda: left_force(step).wait_recv())
         pl.when(has_left)(lambda: right_force(step).wait_recv())
         from_left = fl_in[step]
@@ -385,49 +406,62 @@
     pl.loop(1, groups)(lambda h: far(h).start())
     near(0).start()
     for a in range(nr):
-        out_u[:, a] = u[a]
-    for copy in basis_copies:
-        copy.wait()
-
-    @pl.loop(1, groups)
-    def _(h):
+        final[:, a] = u[a]
+    final_copy = pltpu.make_async_copy(final, out_u, out_s)
+    final_copy.start()
+
+    def add_group(h, total):
+        near(h).wait_recv()
+        j = lax.rem(hi + groups - h, groups)
+        block = [
+            jnp.concatenate([gathered[2 * j, s], gathered[2 * j + 1, s]], axis=0)
+            for s in range(comps)
+        ]
+        return total + dot(left_parts(mix[j]), right_parts(jnp.concatenate(block, axis=1)))
+
+    def next_group(h, total):
         far(h).wait_recv()
         near(h).start()
-
-    for h in range(1, az):
-        adj_copy(h).wait_send()
+        return add_group(h - 1, total)
+
+    coefs = lax.fori_loop(
+        1, groups, next_group, jnp.zeros((3 * cells, comps * width), jnp.float32)
+    )
+    coefs = add_group(groups - 1, coefs)
+    fetches[-1].wait()
+    for h in range(1, az):
         adj_copy(h).wait_recv()
-    pl.loop(0, groups)(lambda h: near(h).wait_recv())
-
-    def block_of(j, s):
-        return jnp.concatenate([gathered[2 * j, s], gathered[2 * j + 1, s]], axis=0)
-
-    def add_pair(j, total):
-        left = halves(mix[j])
-        return tuple(total[s] + dot3(left, halves(block_of(j, s))) for s in range(comps))
-
-    zero = jnp.zeros((3 * cells, width), jnp.float32)
-    coefs = lax.fori_loop(0, groups, add_pair, (zero,) * comps)
+    coefs = [coefs[:, s * width : (s + 1) * width] for s in range(comps)]
     rows = []
     for s in range(comps):
         rows.append(coefs[s][0 : 2 * cells])
         rows.append(swap(coefs[s][2 * cells :]) * ratio)
-    split = halves(jnp.concatenate(rows, axis=0))
+    samples = dot(left_parts(jnp.concatenate(rows, axis=0)), basis[...])
     raw = []
     for h in range(az):
-        r = lax.rem(q + h, az)
-        samples = dot3(split, (bh[r], bl[r]))
         total = jnp.zeros((cells, width), jnp.float32)
         for g in range(3 * comps):
             values = adjoint[g] if h == 0 else adj_all[h, g]
-            total = total + samples[g * cells : (g + 1) * cells] * values
+            at = samples[g * cells : (g + 1) * cells, h * width : (h + 1) * width]
+            total = total + at * values
         raw.append(total)
     raw = jnp.concatenate(raw, axis=1)
     whole = az * width
+    tile_lat = lax.broadcasted_iota(jnp.int32, (depth, width), 0) % lats
     for h in range(az):
-        at = slice(h * width, (h + 1) * width)
-        face_out[0, h] = raw[0:depth, at]
-        face_out[1, h] = raw[cells - depth :, at]
+        low_face = jnp.zeros((depth, width), jnp.float32)
+        high_face = jnp.zeros((depth, width), jnp.float32)
+        for i in range(cells // depth):
+            tile = raw[i * depth : (i + 1) * depth, h * width : (h + 1) * width]
+            first = pltpu.roll(jnp.where(tile_lat == 0, tile, 0.0), i, 0) if i else (
+                jnp.where(tile_lat == 0, tile, 0.0)
+            )
+            low_face = low_face + first
+            turn = (i + depth - (lats - 1)) % depth
+            final_row = jnp.where(tile_lat == lats - 1, tile, 0.0)
+            high_face = high_face + (pltpu.roll(final_row, turn, 0) if turn else final_row)
+        face_out[0, h] = low_face
+        face_out[1, h] = high_face
 
     def face_left(h):
         return remote(
@@ -445,12 +479,12 @@
         pl.when(has_left)(lambda: face_left(h).start())
         pl.when(has_right)(lambda: face_right(h).start())
     level = lax.broadcasted_iota(jnp.int32, (cells, whole), 0)
-    level_in = level % depth
+    lat = level % lats
     around = pltpu.roll(raw, 1, 1) + pltpu.roll(raw, whole - 1, 1)
-    around = around + jnp.where(level_in > 0, pltpu.roll(raw, 1, 0), 0.0)
-    around = around + jnp.where(level_in < depth - 1, pltpu.roll(raw, cells - 1, 0), 0.0)
-    around = around + jnp.where(level >= depth, pltpu.roll(raw, depth, 0), 0.0)
-    around = around + jnp.where(level < cells - depth, pltpu.roll(raw, cells - depth, 0), 0.0)
+    around = around + jnp.where(lat > 0, pltpu.roll(raw, 1, 0), 0.0)
+    around = around + jnp.where(lat < lats - 1, pltpu.roll(raw, cells - 1, 0), 0.0)
+    around = around + jnp.where(level >= lats, pltpu.roll(raw, lats, 0), 0.0)
+    around = around + jnp.where(level < cells - lats, pltpu.roll(raw, cells - lats, 0), 0.0)
     smooth = (1.0 - 6.0 * smooth_rate) * raw + smooth_rate * around
 
     def part_copy(h):
@@ -471,10 +505,25 @@
     below, above = face_in[0, 0], face_in[1, 0]
     for h in range(1, az):
         below, above = below + face_in[0, h], above + face_in[1, h]
-    out_k[...] = result
-    out_k[0:depth] = result[0:depth] + smooth_rate * below
-    out_k[cells - depth :] = out_k[cells - depth :] + smooth_rate * above
-
+    for i in range(cells // depth):
+        turn = (lats - 1 - i) % depth
+        first = pltpu.roll(below, (depth - i) % depth, 0) if i else below
+        final_row = pltpu.roll(above, turn, 0) if turn else above
+        extra = jnp.where(tile_lat == 0, first, 0.0) + jnp.where(
+            tile_lat == lats - 1, final_row, 0.0
+        )
+        at = slice(i * depth, (i + 1) * depth)
+        out_k[at] = result[at] + smooth_rate * extra
+
+    final_copy.wait()
+    pl.when(has_left)(lambda: to_left().wait_send())
+    pl.when(has_right)(lambda: to_right().wait_send())
+    pl.loop(1, n)(lambda h: meta_copy(h).wait_send())
+    for step in range(STEPS):
+        pl.when(has_left)(lambda: left_force(step).wait_send())
+        pl.when(has_right)(lambda: right_force(step).wait_send())
+    for h in range(1, az):
+        adj_copy(h).wait_send()
     for h in range(1, az):
         part_copy(h).wait_send()
     for h in range(az):
@@ -492,48 +541,57 @@
     elements, points = modulus.shape[1], owner.shape[0]
     layers, lats, phi_width = adjoint.shape[1:]
     cells = layers * lats
-    turned = jnp.swapaxes(adjoint, 1, 2).reshape(9, cells, phi_width)
-    high, low = basis_tables(az, width, phi_width)
-    vm, sm = pl.BlockSpec(memory_space=pltpu.VMEM), pl.BlockSpec(memory_space=pltpu.SMEM)
+    assert nr == 5 and cols == 4 * elements and layers == 8 and layers % lats == 0
+    assert points <= width and width == phi_width
+    tiles = np.concatenate(
+        [
+            point_table(elements, cols, width),
+            column_table(elements, cols, width).reshape(-1, cols, width),
+            rim_table(cols, width),
+        ]
+    )
+    basis = basis_tables(az, width, phi_width)
+    vm = pl.BlockSpec(memory_space=pltpu.VMEM)
     anywhere = pl.BlockSpec(memory_space=pl.ANY)
     slot = width // 2
     f32, dma = jnp.float32, pltpu.SemaphoreType.DMA
     buf = lambda *shape: pltpu.VMEM(shape, f32)
+    ints = lambda *shape: pltpu.VMEM(shape, jnp.int32)
     final, smoothed = pl.pallas_call(
         functools.partial(kernel, n, az),
         out_shape=(
             jax.ShapeDtypeStruct(disp.shape, f32),
             jax.ShapeDtypeStruct((cells, phi_width), f32),
         ),
-        in_specs=[vm, vm, sm, sm, sm, sm, sm] + [vm] * 6 + [anywhere] * 2 + [vm] * 3,
-        out_specs=(vm, vm),
+        in_specs=[anywhere] * 15,
+        out_specs=(anywhere, vm),
         scratch_shapes=[
+            buf(*disp.shape), buf(*vel.shape),
+            buf(1, elements), buf(1, elements), buf(1, elements), buf(1, elements),
+            ints(1, elements), ints(2, points), buf(2, points), buf(1, points), ints(1, points),
+            ints(1, points), buf(9, cells, phi_width), pltpu.VMEM(basis.shape[1:], jnp.bfloat16),
+            buf(*tiles.shape), buf(*disp.shape),
             buf(2 * comps + 1, cols, width), buf(2 * comps + 1, cols, width),
             buf(cols, width), buf(cols, width),
             buf(STEPS, comps, cols, width), buf(STEPS, comps, cols, width),
             buf(STEPS, comps, cols, width), buf(STEPS, comps, cols, width),
             buf(n, 8, width), buf(n, comps, slot, width), buf(n // 2 + 1, 3 * cells, width),
             buf(az, 9, cells, phi_width),
-            pltpu.VMEM((az, width, phi_width), jnp.bfloat16),
-            pltpu.VMEM((az, width, phi_width), jnp.bfloat16),
             buf(az, cells, phi_width), buf(az, cells, phi_width),
             buf(2, az, layers, phi_width), buf(2, az, layers, phi_width),
             dma, dma, dma, dma, dma((2, STEPS)), dma((2, STEPS)), dma((n,)), dma((n,)),
             dma((az,)), dma((az,)), dma((n,)), dma((n,)), dma((n,)), dma((n,)),
-            dma((az,)), dma((az,)), dma((2, az)), dma((2, az)), dma((2,)),
+            dma((az,)), dma((az,)), dma((2, az)), dma((2, az)), dma((15,)), dma,
         ],
         compiler_params=pltpu.CompilerParams(
             collective_id=0, has_side_effects=True, vmem_limit_bytes=40 * 1024 * 1024
         ),
     )(
-        disp, vel, modulus, hoop, coupling, density, orders, element, local,
-        scale.reshape(1, points), owner, cell.reshape(1, points), turned,
-        jnp.asarray(high), jnp.asarray(low),
-        jnp.asarray(lane_table(elements, cols, width)),
-        jnp.asarray(column_table(elements, cols, width)),
-        jnp.asarray(rim_table(cols, width)),
-    )
-    return final, jnp.swapaxes(smoothed.reshape(lats, layers, phi_width), 0, 1)
+        disp, vel, modulus, hoop, coupling, density, orders, element.T, local.T,
+        scale.reshape(1, points), owner.T, cell.reshape(1, points),
+        adjoint.reshape(9, cells, phi_width), jnp.asarray(basis), jnp.asarray(tiles),
+    )
+    return final, smoothed.reshape(layers, lats, phi_width)
 
 
 def solution(mesh):

time: 42.4 us -> 48.7 us (1.15)
  local copies, waits for them, and re-layouts: 7.06 us -> 12.7 us
  Pallas kernels: 34.2 us -> 34.9 us
    unnamed x38 -> x32, local copies, waits for them, and re-layouts: 5.43 us -> 12.7 us
    transpose x1 -> x0, local copies, waits for them, and re-layouts: 1.02 us -> none  [on_device(): turned = jnp.swapaxes(adjoint, 1, 2).reshape(9, cells, phi_width)]
    pallas_call x1, Pallas kernels: 34.2 us -> 34.9 us  [on_device(): pl.pallas_call(functools.partial(kernel, n, az), out_shape=(jax.ShapeDtyp...]
    reshape x1 -> x0, local copies, waits for them, and re-layouts: 0.61 us -> none  [on_device(): smoothed.reshape(lats, layers, phi_width)]
where the time goes in v2:
time: 48.7 us; the launch traced here: 48.3 us
  Pallas kernels  34.9 us (72%)
  local copies, waits for them, and re-layouts  12.7 us (26%)
  between operations  0.67 us (1%)
    pallas_call x1, Pallas kernels, on_device(): pl.pallas_call(functools.partial(kernel, n, az), out_shape=(jax.ShapeDtyp...  34.9 us
    unnamed x32, local copies, waits for them, and re-layouts  12.7 us

profile of v2, /device:TPU:0, one launch (start us, length us, event | category | flops | bytes accessed | tf_op | source)
XLA Modules:
  0.0 48.3 jit_solution(10145647112412650040)
XLA Ops:
  0.6 0.0 copy-start
  0.6 1.4 %copy-done = bf16[4,384,512]{2,1,0:T(8,128)(2,1)S(1)} copy-done((bf16[4,384,512]{2,1,0:T(8,128)(2,1)S(1)}, bf16[4,384,512]{2,1,0:T(8,128)(2,1)}, u32[]{:S(2)}) %copy-start) | copy-done | bytes 1572888
  2.0 0.0 copy-start.1
  2.0 0.9 %copy-done.1 = f32[55,8,128]{2,1,0:T(8,128)S(1)} copy-done((f32[55,8,128]{2,1,0:T(8,128)S(1)}, f32[55,8,128]{2,1,0:T(8,128)}, u32[]{:S(2)}) %copy-start.1) | copy-done | bytes 225304
  3.0 0.0 copy-start.2
  3.0 0.9 %copy-done.2 = f32[9,8,4,128]{3,2,1,0:T(4,128)S(1)} copy-done((f32[9,8,4,128]{3,2,1,0:T(4,128)S(1)}, f32[9,8,4,128]{3,2,1,0:T(4,128)}, u32[]{:S(2)}) %copy-start.2) | copy-done | bytes 147480
  3.9 0.0 copy-start.3
  3.9 0.8 %copy-done.3 = f32[3,5,8,128]{3,2,1,0:T(8,128)S(1)} copy-done((f32[3,5,8,128]{3,2,1,0:T(8,128)S(1)}, f32[3,5,8,128]{3,2,1,0:T(8,128)}, u32[]{:S(2)}) %copy-start.3) | copy-done | bytes 61464
  4.7 0.0 copy-start.4
  4.7 0.8 %copy-done.4 = f32[3,5,8,128]{3,2,1,0:T(8,128)S(1)} copy-done((f32[3,5,8,128]{3,2,1,0:T(8,128)S(1)}, f32[3,5,8,128]{3,2,1,0:T(8,128)}, u32[]{:S(2)}) %copy-start.4) | copy-done | bytes 61464
  5.6 0.0 copy-start.5
  5.6 0.7 %copy-done.5 = s32[64,2]{0,1:T(2,128)S(1)} copy-done((s32[64,2]{0,1:T(2,128)S(1)}, s32[64,2]{0,1:T(2,128)}, u32[]{:S(2)}) %copy-start.5) | copy-done | bytes 536
  6.2 0.7 %copy-done.6 = f32[64,2]{0,1:T(2,128)S(1)} copy-done((f32[64,2]{0,1:T(2,128)S(1)}, f32[64,2]{0,1:T(2,128)}, u32[]{:S(2)}) %copy-start.6) | copy-done | bytes 536
  6.9 0.7 %copy-done.7 = f32[1,2]{1,0:T(1,128)S(1)} copy-done((f32[1,2]{1,0:T(1,128)S(1)}, f32[1,2]{1,0:T(1,128)}, u32[]{:S(2)}) %copy-start.7) | copy-done | bytes 32
  7.6 0.7 %copy-done.8 = f32[1,2]{1,0:T(1,128)S(1)} copy-done((f32[1,2]{1,0:T(1,128)S(1)}, f32[1,2]{1,0:T(1,128)}, u32[]{:S(2)}) %copy-start.8) | copy-done | bytes 32
  8.2 0.7 %copy-done.9 = f32[1,2]{1,0:T(1,128)S(1)} copy-done((f32[1,2]{1,0:T(1,128)S(1)}, f32[1,2]{1,0:T(1,128)}, u32[]{:S(2)}) %copy-start.9) | copy-done | bytes 32
  8.9 0.7 %copy-done.10 = f32[1,2]{1,0:T(1,128)S(1)} copy-done((f32[1,2]{1,0:T(1,128)S(1)}, f32[1,2]{1,0:T(1,128)}, u32[]{:S(2)}) %copy-start.10) | copy-done | bytes 32
  9.5 0.7 %copy-done.11 = s32[1,2]{1,0:T(1,128)S(1)} copy-done((s32[1,2]{1,0:T(1,128)S(1)}, s32[1,2]{1,0:T(1,128)}, u32[]{:S(2)}) %copy-start.11) | copy-done | bytes 32
  10.2 0.7 %copy-done.12 = f32[64]{0:T(128)S(1)} copy-done((f32[64]{0:T(128)S(1)}, f32[64]{0:T(128)}, u32[]{:S(2)}) %copy-start.12) | copy-done | bytes 280
  10.8 0.7 %copy-done.13 = s32[64,1]{0,1:T(1,128)S(1)} copy-done((s32[64,1]{0,1:T(1,128)S(1)}, s32[64,1]{0,1:T(1,128)}, u32[]{:S(2)}) %copy-start.13) | copy-done | bytes 280
  11.5 0.7 %copy-done.14 = s32[64]{0:T(128)S(1)} copy-done((s32[64]{0:T(128)S(1)}, s32[64]{0:T(128)}, u32[]{:S(2)}) %copy-start.14) | copy-done | bytes 280
  12.2 34.9 %shard_map.158 = (f32[3,5,8,128]{3,2,1,0:T(8,128)S(1)}, f32[32,128]{1,0:T(8,128)S(1)}) custom-call(f32[3,5,8,128]{3,2,1,0:T(8,128)S(1)} %copy-done.3, f32[3,5,8,128]{3,2,1,0:T(8,128)S(1)} %copy-done.4, f32[1,2]{1,0:T(1,128)S(1)} %copy-done.7, f32[1,2]{1,0:T(1,128)S(1)} %copy-done.8, f32[1,2]{1,0:T(1,128)S(1)} %copy-done.9, f32[1,2]{1,0:T(1,128)S(1)} %copy-done.10, ...), custom_call_target="tpu_custom_call" | custom-call | tf_op jit(solution)/shard_map/pallas_call | solution.py:560
  47.1 0.6 %copy.19 = f32[3,5,8,128]{3,2,1,0:T(8,128)} copy(f32[3,5,8,128]{3,2,1,0:T(8,128)S(1)} %get-tuple-element.8) | data formatting | bytes 122880
  47.7 0.6 %copy.20 = f32[8,4,128]{2,1,0:T(4,128)} copy(f32[8,4,128]{2,1,0:T(4,128)S(1)} %bitcast.8) | data formatting | bytes 32768
  (9 shorter events, 0.0 us)
Async XLA Ops:
  0.6 1.4 %copy-start = (bf16[4,384,512]{2,1,0:T(8,128)(2,1)S(1)}, bf16[4,384,512]{2,1,0:T(8,128)(2,1)}, u32[]{:S(2)}) copy-start(bf16[4,384,512]{2,1,0:T(8,128)(2,1)} %constant.4.clone.basis_a) | copy-start | bytes 4718596
  2.0 0.9 %copy-start.1 = (f32[55,8,128]{2,1,0:T(8,128)S(1)}, f32[55,8,128]{2,1,0:T(8,128)}, u32[]{:S(2)}) copy-start(f32[55,8,128]{2,1,0:T(8,128)} %constant.5.clone.tiles_a) | copy-start | bytes 675844
  3.0 0.9 %copy-start.2 = (f32[9,8,4,128]{3,2,1,0:T(4,128)S(1)}, f32[9,8,4,128]{3,2,1,0:T(4,128)}, u32[]{:S(2)}) copy-start(f32[9,8,4,128]{3,2,1,0:T(4,128)} %param.27) | copy-start | bytes 442372
  3.9 0.8 %copy-start.3 = (f32[3,5,8,128]{3,2,1,0:T(8,128)S(1)}, f32[3,5,8,128]{3,2,1,0:T(8,128)}, u32[]{:S(2)}) copy-start(f32[3,5,8,128]{3,2,1,0:T(8,128)} %disp_a.1) | copy-start | bytes 184324
  4.7 0.8 %copy-start.4 = (f32[3,5,8,128]{3,2,1,0:T(8,128)S(1)}, f32[3,5,8,128]{3,2,1,0:T(8,128)}, u32[]{:S(2)}) copy-start(f32[3,5,8,128]{3,2,1,0:T(8,128)} %vel_a.1) | copy-start | bytes 184324
  5.6 0.7 %copy-start.5 = (s32[64,2]{0,1:T(2,128)S(1)}, s32[64,2]{0,1:T(2,128)}, u32[]{:S(2)}) copy-start(s32[64,2]{0,1:T(2,128)} %param.22) | copy-start | bytes 1540
  6.2 0.7 %copy-start.6 = (f32[64,2]{0,1:T(2,128)S(1)}, f32[64,2]{0,1:T(2,128)}, u32[]{:S(2)}) copy-start(f32[64,2]{0,1:T(2,128)} %param.23) | copy-start | bytes 1540
  6.9 0.7 %copy-start.7 = (f32[1,2]{1,0:T(1,128)S(1)}, f32[1,2]{1,0:T(1,128)}, u32[]{:S(2)}) copy-start(f32[1,2]{1,0:T(1,128)} %modulus_a.1) | copy-start | bytes 28
  7.6 0.7 %copy-start.8 = (f32[1,2]{1,0:T(1,128)S(1)}, f32[1,2]{1,0:T(1,128)}, u32[]{:S(2)}) copy-start(f32[1,2]{1,0:T(1,128)} %hoop_a.1) | copy-start | bytes 28
  8.2 0.7 %copy-start.9 = (f32[1,2]{1,0:T(1,128)S(1)}, f32[1,2]{1,0:T(1,128)}, u32[]{:S(2)}) copy-start(f32[1,2]{1,0:T(1,128)} %coupling_a.1) | copy-start | bytes 28
  8.9 0.7 %copy-start.10 = (f32[1,2]{1,0:T(1,128)S(1)}, f32[1,2]{1,0:T(1,128)}, u32[]{:S(2)}) copy-start(f32[1,2]{1,0:T(1,128)} %density_a.1) | copy-start | bytes 28
  9.5 0.7 %copy-start.11 = (s32[1,2]{1,0:T(1,128)S(1)}, s32[1,2]{1,0:T(1,128)}, u32[]{:S(2)}) copy-start(s32[1,2]{1,0:T(1,128)} %orders_a.1) | copy-start | bytes 28
  10.2 0.7 %copy-start.12 = (f32[64]{0:T(128)S(1)}, f32[64]{0:T(128)}, u32[]{:S(2)}) copy-start(f32[64]{0:T(128)} %param.24) | copy-start | bytes 772
  10.8 0.7 %copy-start.13 = (s32[64,1]{0,1:T(1,128)S(1)}, s32[64,1]{0,1:T(1,128)}, u32[]{:S(2)}) copy-start(s32[64,1]{0,1:T(1,128)} %param.25) | copy-start | bytes 772
  11.5 0.7 %copy-start.14 = (s32[64]{0:T(128)S(1)}, s32[64]{0:T(128)}, u32[]{:S(2)}) copy-start(s32[64]{0:T(128)} %param.26) | copy-start | bytes 772

commit v3 on v2

--- a/solution.py
+++ b/solution.py
@@ -118,7 +118,7 @@
     adjoint, basis, tiles, final,
     halo_out, halo_in, dens_out, dens_in, fl_out, fr_out, fl_in, fr_in, meta, gathered, mix,
     adj_all, part_out, part_in, face_out, face_in,
-    halo_s, halo_r, dens_s, dens_r, f_s, f_r, meta_s, meta_r, adj_s, adj_r, ga_s, ga_r, gb_s, gb_r,
+    halo_s, halo_r, dens_s, dens_r, f_s, f_r, meta_s, meta_r, aa_s, aa_r, ab_s, ab_r, ga_s, ga_r, gb_s, gb_r,
     part_s, part_r, face_s, face_r, in_s, out_s,
 ):
     o, q = lax.axis_index("mer"), lax.axis_index("az")
@@ -226,14 +226,17 @@
 
     pl.loop(1, n)(lambda h: meta_copy(h).start())
 
-    def adj_copy(h):
-        return remote(
-            adjoint, adj_all.at[h], adj_s.at[h], adj_r.at[h], (o, lax.rem(q + az - h, az))
-        )
-
-    fetches[-2].wait()
-    for h in range(1, az):
-        adj_copy(h).start()
+    q_lo, q_hi, q_groups = lax.rem(q, 2), lax.div(q, 2), az // 2
+    q_partner = q_hi * 2 + 1 - q_lo
+
+    def adj_far(h):
+        to = lax.rem(q_hi + h, q_groups) * 2 + q_lo
+        return remote(adjoint, adj_all.at[q], aa_s.at[h], aa_r.at[h], (o, to))
+
+    def adj_near(h):
+        at = lax.rem(q_hi + q_groups - h, q_groups) * 2 + q_lo
+        src = adjoint if h == 0 else adj_all.at[at]
+        return remote(src, adj_all.at[at], ab_s.at[h], ab_r.at[h], (o, q_partner))
 
     order = (q * width + lane) // 2
     ratio = order.astype(jnp.float32) / ORDERS
@@ -377,6 +380,15 @@
         if step == 0:
             pl.loop(1, n)(lambda h: meta_copy(h).wait_recv())
             mix[...] = jnp.zeros_like(mix)
+        if step == 0:
+            fetches[-2].wait()
+            for h in range(1, q_groups):
+                adj_far(h).start()
+            adj_near(0).start()
+        if step == STEPS - 1:
+            for h in range(1, q_groups):
+                adj_far(h).wait_recv()
+                adj_near(h).start()
         mix_blocks(n // 2 * step // STEPS, n // 2 * (step + 1) // STEPS)
         pl.when(has_right)(lambda: left_force(step).wait_recv())
         pl.when(has_left)(lambda: right_force(step).wait_recv())
@@ -429,8 +441,8 @@
     )
     coefs = add_group(groups - 1, coefs)
     fetches[-1].wait()
-    for h in range(1, az):
-        adj_copy(h).wait_recv()
+    for h in range(q_groups):
+        adj_near(h).wait_recv()
     coefs = [coefs[:, s * width : (s + 1) * width] for s in range(comps)]
     rows = []
     for s in range(comps):
@@ -441,7 +453,7 @@
     for h in range(az):
         total = jnp.zeros((cells, width), jnp.float32)
         for g in range(3 * comps):
-            values = adjoint[g] if h == 0 else adj_all[h, g]
+            values = adjoint[g] if h == 0 else adj_all[lax.rem(q + h, az), g]
             at = samples[g * cells : (g + 1) * cells, h * width : (h + 1) * width]
             total = total + at * values
         raw.append(total)
@@ -522,8 +534,10 @@
     for step in range(STEPS):
         pl.when(has_left)(lambda: left_force(step).wait_send())
         pl.when(has_right)(lambda: right_force(step).wait_send())
-    for h in range(1, az):
-        adj_copy(h).wait_send()
+    for h in range(q_groups):
+        adj_near(h).wait_send()
+        if h:
+            adj_far(h).wait_send()
     for h in range(1, az):
         part_copy(h).wait_send()
     for h in range(az):
@@ -552,7 +566,7 @@
     )
     basis = basis_tables(az, width, phi_width)
     vm = pl.BlockSpec(memory_space=pltpu.VMEM)
-    anywhere = pl.BlockSpec(memory_space=pl.ANY)
+    anywhere = pl.BlockSpec(memory_space=pltpu.HBM)
     slot = width // 2
     f32, dma = jnp.float32, pltpu.SemaphoreType.DMA
     buf = lambda *shape: pltpu.VMEM(shape, f32)
@@ -580,11 +594,12 @@
             buf(az, cells, phi_width), buf(az, cells, phi_width),
             buf(2, az, layers, phi_width), buf(2, az, layers, phi_width),
             dma, dma, dma, dma, dma((2, STEPS)), dma((2, STEPS)), dma((n,)), dma((n,)),
-            dma((az,)), dma((az,)), dma((n,)), dma((n,)), dma((n,)), dma((n,)),
+            dma((az,)), dma((az,)), dma((az,)), dma((az,)),
+            dma((n,)), dma((n,)), dma((n,)), dma((n,)),
             dma((az,)), dma((az,)), dma((2, az)), dma((2, az)), dma((15,)), dma,
         ],
         compiler_params=pltpu.CompilerParams(
-            collective_id=0, has_side_effects=True, vmem_limit_bytes=40 * 1024 * 1024
+            collective_id=0, has_side_effects=True, vmem_limit_bytes=60 * 1024 * 1024
         ),
     )(
         disp, vel, modulus, hoop, coupling, density, orders, element.T, local.T,

time: 48.7 us -> 39.1 us (0.80)
  local copies, waits for them, and re-layouts: 12.7 us -> 2.78 us
  Pallas kernels: 34.9 us -> 35.4 us
    unnamed x32 -> x2, local copies, waits for them, and re-layouts: 12.7 us -> 2.78 us
where the time goes in v3:
time: 39.1 us; the launch traced here: 38.8 us
  Pallas kernels  35.4 us (91%)
  local copies, waits for them, and re-layouts  2.78 us (7%)
  between operations  0.64 us (2%)
    pallas_call x1, Pallas kernels, on_device(): pl.pallas_call(functools.partial(kernel, n, az), out_shape=(jax.ShapeDtyp...  35.4 us
    unnamed x2, local copies, waits for them, and re-layouts  2.78 us

profile of v3, /device:TPU:0, one launch (start us, length us, event | category | flops | bytes accessed | tf_op | source)
XLA Modules:
  0.0 38.8 jit_solution(16710728142844565184)
XLA Ops:
  0.6 35.4 %shard_map.158 = (f32[3,5,8,128]{3,2,1,0:T(8,128)}, f32[32,128]{1,0:T(8,128)}) custom-call(f32[3,5,8,128]{3,2,1,0:T(8,128)} %disp_a.1, f32[3,5,8,128]{3,2,1,0:T(8,128)} %vel_a.1, f32[1,2]{1,0:T(1,128)} %modulus_a.1, f32[1,2]{1,0:T(1,128)} %hoop_a.1, f32[1,2]{1,0:T(1,128)} %coupling_a.1, f32[1,2]{1,0:T(1,128)} %density_a.1, s32[1,2]{1,0:T(1,128)} %orders_a.1, ...), custom_call_target="tpu_custom_call" | custom-call | tf_op jit(solution)/shard_map/pallas_call | solution.py:574
  36.1 1.5 %copy.19 = f32[3,5,8,128]{3,2,1,0:T(8,128)} copy(f32[3,5,8,128]{3,2,1,0:T(8,128)} %get-tuple-element.8) | data formatting | bytes 122880
  37.5 1.3 %copy.20 = f32[8,4,128]{2,1,0:T(4,128)} copy(f32[8,4,128]{2,1,0:T(4,128)} %bitcast.8) | data formatting | bytes 32768

commit v4 on v3

--- a/solution.py
+++ b/solution.py
@@ -114,15 +114,16 @@
 def kernel(
     n, az, disp_a, vel_a, modulus_a, hoop_a, coupling_a, density_a, orders_a, element_a, local_a,
     scale_a, owner_a, cell_a, adjoint_a, basis_a, tiles_a, out_u, out_k,
-    disp, vel, modulus, hoop, coupling, density, orders, element, local, scale, owner, cell,
-    adjoint, basis, tiles, final,
-    halo_out, halo_in, dens_out, dens_in, fl_out, fr_out, fl_in, fr_in, meta, gathered, mix,
+    modulus, hoop, coupling, density, orders, element, local, scale, owner, cell,
+    adjoint, basis, tiles,
+    halo_out, halo_in, edge_out, edge_in, force_out, force_in, meta, gathered, mix,
     adj_all, part_out, part_in, face_out, face_in,
-    halo_s, halo_r, dens_s, dens_r, f_s, f_r, meta_s, meta_r, aa_s, aa_r, ab_s, ab_r, ga_s, ga_r, gb_s, gb_r,
-    part_s, part_r, face_s, face_r, in_s, out_s,
+    halo_s, halo_r, edge_s, edge_r, f_s, f_r, meta_s, meta_r, aa_s, aa_r, ab_s, ab_r, ga_s, ga_r, gb_s, gb_r,
+    part_s, part_r, face_s, face_r, in_s,
 ):
     o, q = lax.axis_index("mer"), lax.axis_index("az")
-    comps, nr, cols, width = disp.shape
+    comps, nr, cols, width = out_u.shape
+    fields = comps * nr
     elements = modulus.shape[1]
     points = owner.shape[1]
     slot = gathered.shape[2]
@@ -132,8 +133,9 @@
     lats = cells // depth
     weights, _, _, stiffness = gll_tables()
     has_left, has_right = o > 0, o < n - 1
+    has_left_2, has_right_2 = o > 1, o < n - 2
     pairs = [
-        (disp_a, disp), (vel_a, vel), (modulus_a, modulus), (hoop_a, hoop), (coupling_a, coupling),
+        (disp_a, halo_out.at[0:fields]), (vel_a, halo_out.at[fields : 2 * fields]), (modulus_a, modulus), (hoop_a, hoop), (coupling_a, coupling),
         (density_a, density), (orders_a, orders), (element_a, element), (local_a, local),
         (scale_a, scale), (owner_a, owner), (cell_a, cell), (tiles_a, tiles), (adjoint_a, adjoint),
         (basis_a.at[q], basis),
@@ -143,9 +145,8 @@
         fetch.start()
 
     halo_in[...] = jnp.zeros_like(halo_in)
-    dens_in[...] = jnp.zeros_like(dens_in)
-    fl_in[...] = jnp.zeros_like(fl_in)
-    fr_in[...] = jnp.zeros_like(fr_in)
+    edge_in[...] = jnp.zeros_like(edge_in)
+    force_in[...] = jnp.zeros_like(force_in)
     face_in[...] = jnp.zeros_like(face_in)
     gathered[:, :, nodes:, :] = jnp.zeros((n, comps, slot - nodes, width), jnp.float32)
 
@@ -172,8 +173,12 @@
 
     row = lax.broadcasted_iota(jnp.int32, (cols, width), 0)
     lane = lax.broadcasted_iota(jnp.int32, (1, width), 1)
-    u = [disp[:, a] for a in range(nr)]
-    v = [vel[:, a] for a in range(nr)]
+
+    def field(ref, kind):
+        at = lambda s, a: ref[kind * fields + s * nr + a]
+        return [jnp.stack([at(s, a) for s in range(comps)]) for a in range(nr)]
+
+    u, v = field(halo_out, 0), field(halo_out, 1)
 
     def first_column(values):
         total = jnp.zeros((comps, cols, width), jnp.float32)
@@ -181,12 +186,16 @@
             total = jnp.where((row == a)[None], values[a][:, 0:1, :], total)
         return total
 
-    halo_out[0:comps] = first_column(u)
-    halo_out[comps : 2 * comps] = first_column(v)
-    halo_out[2 * comps] = jnp.broadcast_to(density[0:1, 0:1], (cols, width))
-    dens_out[...] = jnp.broadcast_to(
-        density[0:1, elements - 1 : elements], (cols, width)
-    )
+    edge_out[0:comps] = first_column(u)
+    edge_out[comps:] = first_column(v)
+    one = lambda ref, e: ref[0:1, e : e + 1].astype(jnp.float32)
+    known = jnp.zeros((2 * cols, width), jnp.float32)
+    row_2 = lax.broadcasted_iota(jnp.int32, (2 * cols, width), 0)
+    for i, ref in enumerate((modulus, hoop, coupling, density, orders)):
+        for e in range(elements):
+            known = jnp.where(row_2 == 5 * e + i, one(ref, e), known)
+    halo_out[2 * fields] = known[0:cols]
+    halo_out[2 * fields + 1] = known[cols:]
     spare = jnp.zeros((1, width - points), jnp.float32) if width > points else None
 
     def wide(line):
@@ -216,15 +225,22 @@
             device_id=device, device_id_type=MESH,
         )
 
-    to_left = lambda: remote(halo_out, halo_in, halo_s, halo_r, (o - 1, q))
-    to_right = lambda: remote(dens_out, dens_in, dens_s, dens_r, (o + 1, q))
+    def to_left():
+        return remote(halo_out, halo_in.at[1], halo_s.at[0], halo_r.at[0], (o - 1, q))
+
+    def to_right():
+        return remote(halo_out, halo_in.at[0], halo_s.at[1], halo_r.at[1], (o + 1, q))
+
+    def to_left_2():
+        return remote(edge_out, edge_in, edge_s, edge_r, (o - 2, q))
+
+    def meta_copy(h):
+        return remote(meta.at[o], meta.at[o], meta_s.at[h], meta_r.at[h], (lax.rem(o + h, n), q))
+
+    pl.loop(1, n)(lambda h: meta_copy(h).start())
     pl.when(has_left)(lambda: to_left().start())
     pl.when(has_right)(lambda: to_right().start())
-
-    def meta_copy(h):
-        return remote(meta.at[o], meta.at[o], meta_s.at[h], meta_r.at[h], (lax.rem(o + h, n), q))
-
-    pl.loop(1, n)(lambda h: meta_copy(h).start())
+    pl.when(has_left_2)(lambda: to_left_2().start())
 
     q_lo, q_hi, q_groups = lax.rem(q, 2), lax.div(q, 2), az // 2
     q_partner = q_hi * 2 + 1 - q_lo
@@ -238,53 +254,56 @@
         src = adjoint if h == 0 else adj_all.at[at]
         return remote(src, adj_all.at[at], ab_s.at[h], ab_r.at[h], (o, q_partner))
 
+    fetches[-2].wait()
+    for h in range(1, q_groups):
+        adj_far(h).start()
+    adj_near(0).start()
+
     order = (q * width + lane) // 2
     ratio = order.astype(jnp.float32) / ORDERS
     even = (lane % 2 == 0)
-    one = lambda ref, e: ref[0:1, e : e + 1]
-    keep = [jnp.where(order < one(orders, e), 1.0, 0.0) for e in range(elements)]
-    mod = [one(modulus, e) * keep[e] for e in range(elements)]
-    hp = [one(hoop, e) * keep[e] * (ratio * ratio) for e in range(elements)]
-    cp = [one(coupling, e) * keep[e] * ratio for e in range(elements)]
+    last = elements - 1
+    w_end = float(weights[4])
     points_at = 0
     cols_at = 9 * (1 + elements)
     rim_at = cols_at + elements * (cols + 2)
     cols_t = lambda e, which: tiles[cols_at + e * (cols + 2) + which]
-    last = elements - 1
-    w_end = float(weights[4])
-
-    def blend(per_element, which):
-        total = per_element[0] * cols_t(0, which)
-        for e in range(1, elements):
-            total = total + per_element[e] * cols_t(e, which)
-        return total
-
-    c_radial, c_hoop, c_pair = blend(mod, 0), blend(hp, 0), blend(cp, 0)
-    c_colat = [blend(mod, 1 + d) for d in range(cols)]
-    c_rim = mod[last] * cols_t(last, cols + 1)
     w_rim = jnp.zeros((cols, width), jnp.float32)
     for a in range(nr):
         w_rim = jnp.where(row == a, float(weights[a]), w_rim)
-    r_radial = [mod[last] * w_end * tiles[rim_at + d] for d in range(cols)]
-    r_radial[0] = r_radial[0] + w_rim * (
-        mod[last] * float(stiffness[4, 4]) + hp[last] * w_end
-    )
-    r_pair = w_rim * (cp[last] * w_end)
-
-    pl.when(has_right)(lambda: to_left().wait_recv())
-    pl.when(has_left)(lambda: to_right().wait_recv())
-    col_mass = one(density, 0) * cols_t(0, 0)
-    for e in range(1, elements):
-        col_mass = col_mass + one(density, e) * cols_t(e, 0)
-    col_mass = col_mass + jnp.where(row == 0, w_end * dens_in[...], 0.0)
-    rim_mass = w_end * (one(density, last) + halo_in[2 * comps])
-    inv_main = [step_scale / (float(weights[a]) * col_mass) for a in range(nr)]
-    inv_rim = step_scale / (jnp.where(row < nr, w_rim, 1.0) * rim_mass)
-    inv_rim = jnp.where(has_right, inv_rim, 0.0)
-
-    rim = halo_in[0:comps]
-    rim_before = rim - halo_in[comps : 2 * comps]
-    before = [u[a] - v[a] for a in range(nr)]
+
+    def setup(ref, before, there):
+        def value(i, e):
+            at = 5 * e + i
+            return ref[2 * fields + at // cols, at % cols : at % cols + 1, :]
+
+        def blend(per_element, which):
+            total = per_element[0] * cols_t(0, which)
+            for e in range(1, elements):
+                total = total + per_element[e] * cols_t(e, which)
+            return total
+
+        keep = [jnp.where(order.astype(jnp.float32) < value(4, e), 1.0, 0.0) for e in range(elements)]
+        mod = [value(0, e) * keep[e] for e in range(elements)]
+        hp = [value(1, e) * keep[e] * (ratio * ratio) for e in range(elements)]
+        cp = [value(2, e) * keep[e] * ratio for e in range(elements)]
+        c_radial, c_hoop, c_pair = blend(mod, 0), blend(hp, 0), blend(cp, 0)
+        c_colat = [blend(mod, 1 + d) for d in range(cols)]
+        c_rim = mod[last] * cols_t(last, cols + 1)
+        r_radial = [mod[last] * w_end * tiles[rim_at + d] for d in range(cols)]
+        r_radial[0] = r_radial[0] + w_rim * (
+            mod[last] * float(stiffness[4, 4]) + hp[last] * w_end
+        )
+        r_pair = w_rim * (cp[last] * w_end)
+        mass = blend([value(3, e) for e in range(elements)], 0)
+        if before is not None:
+            at = 5 * last + 3
+            shared = before[2 * fields + at // cols, at % cols : at % cols + 1, :]
+            mass = mass + jnp.where(row == 0, w_end * shared, 0.0)
+        inverse = [step_scale / (float(weights[a]) * mass) for a in range(nr)]
+        if there is not None:
+            inverse = [jnp.where(there, x, 0.0) for x in inverse]
+        return (c_radial, c_hoop, c_pair, c_colat, c_rim, r_radial, r_pair), inverse
 
     def swap(x):
         axis = x.ndim - 1
@@ -295,11 +314,44 @@
             [factor * swap(x[2]), jnp.zeros((cols, width), jnp.float32), -factor * swap(x[0])]
         )
 
-    def left_force(step):
-        return remote(fl_out.at[step], fr_in.at[step], f_s.at[0, step], f_r.at[0, step], (o - 1, q))
-
-    def right_force(step):
-        return remote(fr_out.at[step], fl_in.at[step], f_s.at[1, step], f_r.at[1, step], (o + 1, q))
+    def force_copy():
+        return remote(force_out, force_in, f_s, f_r, (o + 1, q))
+
+    def main_force(u, rim, coefs):
+        c_radial, c_hoop, c_pair, c_colat, c_rim, _, _ = coefs
+        forces = []
+        for a in range(nr):
+            w_a = float(weights[a])
+            colat = c_rim * rim[:, a : a + 1, :] + c_colat[0] * u[a]
+            for d in range(1, cols):
+                colat = colat + c_colat[d] * pltpu.roll(u[a], d, 1)
+            radial = float(stiffness[a, 0]) * u[0]
+            for i in range(1, nr):
+                radial = radial + float(stiffness[a, i]) * u[i]
+            force = pair(u[a], w_a * c_pair) - (
+                c_radial * radial + w_a * (colat + c_hoop * u[a])
+            )
+            forces.append(force)
+        return forces
+
+    def end_force(u, rim, coefs):
+        c_rim, r_radial, r_pair = coefs[4:]
+        force = jnp.zeros((comps, cols, width), jnp.float32)
+        for a in range(nr):
+            ending = jnp.sum(c_rim * u[a], axis=1, keepdims=True)
+            force = jnp.where((row == a)[None], -float(weights[a]) * ending, force)
+        force = force + pair(rim, r_pair)
+        for d in range(cols):
+            force = force - r_radial[d] * (pltpu.roll(rim, d, 1) if d else rim)
+        return force
+
+    def with_edge(forces, edge):
+        return [
+            forces[a] + jnp.where((row == 0)[None], edge[:, a : a + 1, :], 0.0) for a in range(nr)
+        ]
+
+    def advance(u, before, forces, inverse):
+        return [2.0 * u[a] - before[a] + inverse[a] * forces[a] for a in range(nr)]
 
     wanted = lax.broadcasted_iota(jnp.int32, (cells, width), 0).astype(jnp.float32)
     upper = lane >= slot
@@ -353,53 +405,46 @@
             mix[j] = mix[j] + first + jnp.where(upper, second, 0.0)
             mix[j + 1] = mix[j + 1] + jnp.where(upper, 0.0, second)
 
-    for step in range(STEPS):
-        forces, rim_force = [], jnp.zeros((comps, cols, width), jnp.float32)
-        for a in range(nr):
-            w_a = float(weights[a])
-            colat = c_rim * rim[:, a : a + 1, :] + c_colat[0] * u[a]
-            for d in range(1, cols):
-                colat = colat + c_colat[d] * pltpu.roll(u[a], d, 1)
-            radial = float(stiffness[a, 0]) * u[0]
-            for i in range(1, nr):
-                radial = radial + float(stiffness[a, i]) * u[i]
-            force = pair(u[a], w_a * c_pair) - (
-                c_radial * radial + w_a * (colat + c_hoop * u[a])
-            )
-            forces.append(force)
-            ending = jnp.sum(c_rim * u[a], axis=1, keepdims=True)
-            rim_force = jnp.where((row == a)[None], -w_a * ending, rim_force)
-        rim_force = rim_force + pair(rim, r_pair)
-        for d in range(cols):
-            rim_force = rim_force - r_radial[d] * (pltpu.roll(rim, d, 1) if d else rim)
-        fl_out[step] = first_column(forces)
-        fr_out[step] = rim_force
-        pl.when(has_left)(lambda: left_force(step).start())
-        pl.when(has_right)(lambda: right_force(step).start())
-        ahead = [2.0 * u[a] - before[a] + inv_main[a] * forces[a] for a in range(nr)]
-        if step == 0:
-            pl.loop(1, n)(lambda h: meta_copy(h).wait_recv())
-            mix[...] = jnp.zeros_like(mix)
-        if step == 0:
-            fetches[-2].wait()
-            for h in range(1, q_groups):
-                adj_far(h).start()
-            adj_near(0).start()
-        if step == STEPS - 1:
-            for h in range(1, q_groups):
-                adj_far(h).wait_recv()
-                adj_near(h).start()
-        mix_blocks(n // 2 * step // STEPS, n // 2 * (step + 1) // STEPS)
-        pl.when(has_right)(lambda: left_force(step).wait_recv())
-        pl.when(has_left)(lambda: right_force(step).wait_recv())
-        from_left = fl_in[step]
-        for a in range(nr):
-            ahead[a] = ahead[a] + jnp.where(
-                (row == 0)[None], inv_main[a] * from_left[:, a : a + 1, :], 0.0
-            )
-        rim_ahead = 2.0 * rim - rim_before + inv_rim * (rim_force + fr_in[step])
-        rim_ahead = jnp.where(has_right, rim_ahead, 0.0)
-        before, u, rim_before, rim = u, ahead, rim, rim_ahead
+    pl.loop(1, n)(lambda h: meta_copy(h).wait_recv())
+    mix[...] = jnp.zeros_like(mix)
+    mix_blocks(0, n // 2)
+
+    pl.when(has_right)(lambda: to_left().wait_recv())
+    pl.when(has_left)(lambda: to_right().wait_recv())
+    pl.when(has_right_2)(lambda: to_left_2().wait_recv())
+    left, right = halo_in.at[0], halo_in.at[1]
+    coefs_l, inverse_l = setup(left, None, has_left)
+    coefs_m, inverse_m = setup(halo_out, left, None)
+    coefs_r, inverse_r = setup(right, halo_out, has_right)
+    u_l, u_r = field(left, 0), field(right, 0)
+    before_l = [x - y for x, y in zip(u_l, field(left, 1))]
+    before = [x - y for x, y in zip(u, v)]
+    before_r = [x - y for x, y in zip(u_r, field(right, 1))]
+    far_rim = edge_in[0:comps]
+
+    rim_l, rim = first_column(u), first_column(u_r)
+    force_l = main_force(u_l, rim_l, coefs_l)
+    force_m = with_edge(main_force(u, rim, coefs_m), end_force(u_l, rim_l, coefs_l))
+    force_r = with_edge(main_force(u_r, far_rim, coefs_r), end_force(u, rim, coefs_m))
+    u_l = advance(u_l, before_l, force_l, inverse_l)
+    before, u = u, advance(u, before, force_m, inverse_m)
+    before_r, u_r = u_r, advance(u_r, before_r, force_r, inverse_r)
+
+    rim_l, rim = first_column(u), first_column(u_r)
+    force_m = with_edge(main_force(u, rim, coefs_m), end_force(u_l, rim_l, coefs_l))
+    force_r = with_edge(main_force(u_r, far_rim, coefs_r), end_force(u, rim, coefs_m))
+    before, u = u, advance(u, before, force_m, inverse_m)
+    u_r = advance(u_r, before_r, force_r, inverse_r)
+
+    rim = first_column(u_r)
+    force_out[...] = end_force(u, rim, coefs_m)
+    pl.when(has_right)(lambda: force_copy().start())
+    force_m = main_force(u, rim, coefs_m)
+    for h in range(1, q_groups):
+        adj_far(h).wait_recv()
+        adj_near(h).start()
+    pl.when(has_left)(lambda: force_copy().wait_recv())
+    u = advance(u, before, with_edge(force_m, force_in[...]), inverse_m)
 
     for a in range(nr):
         gathered[o, :, a * cols : (a + 1) * cols, :] = u[a]
@@ -418,9 +463,7 @@
     pl.loop(1, groups)(lambda h: far(h).start())
     near(0).start()
     for a in range(nr):
-        final[:, a] = u[a]
-    final_copy = pltpu.make_async_copy(final, out_u, out_s)
-    final_copy.start()
+        out_u[:, a] = u[a]
 
     def add_group(h, total):
         near(h).wait_recv()
@@ -527,13 +570,11 @@
         at = slice(i * depth, (i + 1) * depth)
         out_k[at] = result[at] + smooth_rate * extra
 
-    final_copy.wait()
     pl.when(has_left)(lambda: to_left().wait_send())
     pl.when(has_right)(lambda: to_right().wait_send())
     pl.loop(1, n)(lambda h: meta_copy(h).wait_send())
-    for step in range(STEPS):
-        pl.when(has_left)(lambda: left_force(step).wait_send())
-        pl.when(has_right)(lambda: right_force(step).wait_send())
+    pl.when(has_left_2)(lambda: to_left_2().wait_send())
+    pl.when(has_right)(lambda: force_copy().wait_send())
     for h in range(q_groups):
         adj_near(h).wait_send()
         if h:
@@ -555,6 +596,7 @@
     elements, points = modulus.shape[1], owner.shape[0]
     layers, lats, phi_width = adjoint.shape[1:]
     cells = layers * lats
+    assert STEPS == 3 and elements == 2
     assert nr == 5 and cols == 4 * elements and layers == 8 and layers % lats == 0
     assert points <= width and width == phi_width
     tiles = np.concatenate(
@@ -574,37 +616,41 @@
     final, smoothed = pl.pallas_call(
         functools.partial(kernel, n, az),
         out_shape=(
-            jax.ShapeDtypeStruct(disp.shape, f32),
-            jax.ShapeDtypeStruct((cells, phi_width), f32),
+            pltpu.VMEM(disp.shape, f32),
+            pltpu.VMEM((cells, phi_width), f32),
         ),
         in_specs=[anywhere] * 15,
-        out_specs=(anywhere, vm),
+        out_specs=(vm, vm),
         scratch_shapes=[
-            buf(*disp.shape), buf(*vel.shape),
             buf(1, elements), buf(1, elements), buf(1, elements), buf(1, elements),
             ints(1, elements), ints(2, points), buf(2, points), buf(1, points), ints(1, points),
             ints(1, points), buf(9, cells, phi_width), pltpu.VMEM(basis.shape[1:], jnp.bfloat16),
-            buf(*tiles.shape), buf(*disp.shape),
-            buf(2 * comps + 1, cols, width), buf(2 * comps + 1, cols, width),
-            buf(cols, width), buf(cols, width),
-            buf(STEPS, comps, cols, width), buf(STEPS, comps, cols, width),
-            buf(STEPS, comps, cols, width), buf(STEPS, comps, cols, width),
+            buf(*tiles.shape),
+            buf(2 * comps * nr + 2, cols, width), buf(2, 2 * comps * nr + 2, cols, width),
+            buf(2 * comps, cols, width), buf(2 * comps, cols, width),
+            buf(comps, cols, width), buf(comps, cols, width),
             buf(n, 8, width), buf(n, comps, slot, width), buf(n // 2 + 1, 3 * cells, width),
             buf(az, 9, cells, phi_width),
             buf(az, cells, phi_width), buf(az, cells, phi_width),
             buf(2, az, layers, phi_width), buf(2, az, layers, phi_width),
-            dma, dma, dma, dma, dma((2, STEPS)), dma((2, STEPS)), dma((n,)), dma((n,)),
+            dma((2,)), dma((2,)), dma, dma, dma, dma, dma((n,)), dma((n,)),
             dma((az,)), dma((az,)), dma((az,)), dma((az,)),
             dma((n,)), dma((n,)), dma((n,)), dma((n,)),
-            dma((az,)), dma((az,)), dma((2, az)), dma((2, az)), dma((15,)), dma,
+            dma((az,)), dma((az,)), dma((2, az)), dma((2, az)), dma((15,)),
         ],
         compiler_params=pltpu.CompilerParams(
-            collective_id=0, has_side_effects=True, vmem_limit_bytes=60 * 1024 * 1024
+            collective_id=0, has_side_effects=True, vmem_limit_bytes=40 * 1024 * 1024
         ),
     )(
-        disp, vel, modulus, hoop, coupling, density, orders, element.T, local.T,
-        scale.reshape(1, points), owner.T, cell.reshape(1, points),
-        adjoint.reshape(9, cells, phi_width), jnp.asarray(basis), jnp.asarray(tiles),
+        *(
+            pltpu.with_memory_space_constraint(x, pltpu.HBM)
+            for x in (
+                disp.reshape(comps * nr, cols, width), vel.reshape(comps * nr, cols, width),
+                modulus, hoop, coupling, density, orders, element.T, local.T,
+                scale.reshape(1, points), owner.T, cell.reshape(1, points),
+                adjoint.reshape(9, cells, phi_width), jnp.asarray(basis), jnp.asarray(tiles),
+            )
+        )
     )
     return final, smoothed.reshape(layers, lats, phi_width)
 

time: 39.1 us -> 34.9 us (0.89)
  Pallas kernels: 35.4 us -> 32.9 us
  local copies, waits for them, and re-layouts: 2.78 us -> 1.23 us
    pallas_call x1, Pallas kernels: 35.4 us -> 32.9 us  [on_device(): pl.pallas_call(functools.partial(kernel, n, az), out_shape=(pltpu.VMEM(di...]
    unnamed x2, local copies, waits for them, and re-layouts: 2.78 us -> 1.23 us
where the time goes in v4:
time: 34.9 us; the launch traced here: 34.8 us
  Pallas kernels  32.9 us (94%)
  local copies, waits for them, and re-layouts  1.23 us (4%)
  between operations  0.64 us (2%)
    pallas_call x1, Pallas kernels, on_device(): pl.pallas_call(functools.partial(kernel, n, az), out_shape=(pltpu.VMEM(di...  32.9 us
    unnamed x2, local copies, waits for them, and re-layouts  1.23 us

profile of v4, /device:TPU:0, one launch (start us, length us, event | category | flops | bytes accessed | tf_op | source)
XLA Modules:
  0.0 34.8 jit_solution(13842742260740807721)
XLA Ops:
  0.6 32.9 %shard_map.158 = (f32[3,5,8,128]{3,2,1,0:T(8,128)S(1)}, f32[32,128]{1,0:T(8,128)S(1)}) custom-call(f32[15,8,128]{2,1,0:T(8,128)} %bitcast.11, f32[15,8,128]{2,1,0:T(8,128)} %bitcast.12, f32[1,2]{1,0:T(1,128)} %modulus_a.1, f32[1,2]{1,0:T(1,128)} %hoop_a.1, f32[1,2]{1,0:T(1,128)} %coupling_a.1, f32[1,2]{1,0:T(1,128)} %density_a.1, s32[1,2]{1,0:T(1,128)} %orders_a.1, ...), custom_call_target="tpu_custom_call" | custom-call | tf_op jit(solution)/shard_map/pallas_call | solution.py:616
  33.5 0.6 %copy.19 = f32[3,5,8,128]{3,2,1,0:T(8,128)} copy(f32[3,5,8,128]{3,2,1,0:T(8,128)S(1)} %get-tuple-element.6) | data formatting | bytes 122880
  34.2 0.6 %copy.20 = f32[8,4,128]{2,1,0:T(4,128)} copy(f32[8,4,128]{2,1,0:T(4,128)S(1)} %bitcast.9) | data formatting | bytes 32768

commit v5 on v4

--- a/solution.py
+++ b/solution.py
@@ -116,7 +116,7 @@
     scale_a, owner_a, cell_a, adjoint_a, basis_a, tiles_a, out_u, out_k,
     modulus, hoop, coupling, density, orders, element, local, scale, owner, cell,
     adjoint, basis, tiles,
-    halo_out, halo_in, edge_out, edge_in, force_out, force_in, meta, gathered, mix,
+    halo_out, halo_in, edge_out, edge_in, half_out, half_in, meta, gathered, mix,
     adj_all, part_out, part_in, face_out, face_in,
     halo_s, halo_r, edge_s, edge_r, f_s, f_r, meta_s, meta_r, aa_s, aa_r, ab_s, ab_r, ga_s, ga_r, gb_s, gb_r,
     part_s, part_r, face_s, face_r, in_s,
@@ -146,7 +146,7 @@
 
     halo_in[...] = jnp.zeros_like(halo_in)
     edge_in[...] = jnp.zeros_like(edge_in)
-    force_in[...] = jnp.zeros_like(force_in)
+    half_in[...] = jnp.zeros_like(half_in)
     face_in[...] = jnp.zeros_like(face_in)
     gathered[:, :, nodes:, :] = jnp.zeros((n, comps, slot - nodes, width), jnp.float32)
 
@@ -196,6 +196,16 @@
             known = jnp.where(row_2 == 5 * e + i, one(ref, e), known)
     halo_out[2 * fields] = known[0:cols]
     halo_out[2 * fields + 1] = known[cols:]
+    halves_at = (fields + 1) // 2
+    for k in range(halves_at):
+        tile = halo_out[k]
+        if k + halves_at < fields:
+            tile = jnp.where(
+                row >= cols // 2, tile, pltpu.roll(halo_out[k + halves_at], cols // 2, 0)
+            )
+        half_out[k] = tile
+    half_out[halves_at] = known[0:cols]
+    half_out[halves_at + 1] = known[cols:]
     spare = jnp.zeros((1, width - points), jnp.float32) if width > points else None
 
     def wide(line):
@@ -231,6 +241,9 @@
     def to_right():
         return remote(halo_out, halo_in.at[0], halo_s.at[1], halo_r.at[1], (o + 1, q))
 
+    def to_right_2():
+        return remote(half_out, half_in, f_s, f_r, (o + 2, q))
+
     def to_left_2():
         return remote(edge_out, edge_in, edge_s, edge_r, (o - 2, q))
 
@@ -241,6 +254,7 @@
     pl.when(has_left)(lambda: to_left().start())
     pl.when(has_right)(lambda: to_right().start())
     pl.when(has_left_2)(lambda: to_left_2().start())
+    pl.when(has_right_2)(lambda: to_right_2().start())
 
     q_lo, q_hi, q_groups = lax.rem(q, 2), lax.div(q, 2), az // 2
     q_partner = q_hi * 2 + 1 - q_lo
@@ -272,10 +286,10 @@
     for a in range(nr):
         w_rim = jnp.where(row == a, float(weights[a]), w_rim)
 
-    def setup(ref, before, there):
+    def setup(ref, base, before, there):
         def value(i, e):
             at = 5 * e + i
-            return ref[2 * fields + at // cols, at % cols : at % cols + 1, :]
+            return ref[base + at // cols, at % cols : at % cols + 1, :]
 
         def blend(per_element, which):
             total = per_element[0] * cols_t(0, which)
@@ -298,7 +312,8 @@
         mass = blend([value(3, e) for e in range(elements)], 0)
         if before is not None:
             at = 5 * last + 3
-            shared = before[2 * fields + at // cols, at % cols : at % cols + 1, :]
+            ref_2, base_2 = before
+            shared = ref_2[base_2 + at // cols, at % cols : at % cols + 1, :]
             mass = mass + jnp.where(row == 0, w_end * shared, 0.0)
         inverse = [step_scale / (float(weights[a]) * mass) for a in range(nr)]
         if there is not None:
@@ -313,9 +328,6 @@
         return jnp.stack(
             [factor * swap(x[2]), jnp.zeros((cols, width), jnp.float32), -factor * swap(x[0])]
         )
-
-    def force_copy():
-        return remote(force_out, force_in, f_s, f_r, (o + 1, q))
 
     def main_force(u, rim, coefs):
         c_radial, c_hoop, c_pair, c_colat, c_rim, _, _ = coefs
@@ -412,10 +424,16 @@
     pl.when(has_right)(lambda: to_left().wait_recv())
     pl.when(has_left)(lambda: to_right().wait_recv())
     pl.when(has_right_2)(lambda: to_left_2().wait_recv())
+    pl.when(has_left_2)(lambda: to_right_2().wait_recv())
     left, right = halo_in.at[0], halo_in.at[1]
-    coefs_l, inverse_l = setup(left, None, has_left)
-    coefs_m, inverse_m = setup(halo_out, left, None)
-    coefs_r, inverse_r = setup(right, halo_out, has_right)
+    known_at = 2 * fields
+    coefs_ll, _ = setup(half_in, halves_at, None, has_left_2)
+    coefs_l, inverse_l = setup(left, known_at, (half_in, halves_at), has_left)
+    coefs_m, inverse_m = setup(halo_out, known_at, (left, known_at), None)
+    coefs_r, inverse_r = setup(right, known_at, (halo_out, known_at), has_right)
+    half_tiles = [half_in[k] for k in range(halves_at)]
+    half_tiles += [pltpu.roll(half_in[k], cols // 2, 0) for k in range(fields - halves_at)]
+    u_ll = [jnp.stack([half_tiles[s * nr + a] for s in range(comps)]) for a in range(nr)]
     u_l, u_r = field(left, 0), field(right, 0)
     before_l = [x - y for x, y in zip(u_l, field(left, 1))]
     before = [x - y for x, y in zip(u, v)]
@@ -423,10 +441,12 @@
     far_rim = edge_in[0:comps]
 
     rim_l, rim = first_column(u), first_column(u_r)
-    force_l = main_force(u_l, rim_l, coefs_l)
+    force_l = with_edge(
+        main_force(u_l, rim_l, coefs_l), end_force(u_ll, first_column(u_l), coefs_ll)
+    )
     force_m = with_edge(main_force(u, rim, coefs_m), end_force(u_l, rim_l, coefs_l))
     force_r = with_edge(main_force(u_r, far_rim, coefs_r), end_force(u, rim, coefs_m))
-    u_l = advance(u_l, before_l, force_l, inverse_l)
+    before_l, u_l = u_l, advance(u_l, before_l, force_l, inverse_l)
     before, u = u, advance(u, before, force_m, inverse_m)
     before_r, u_r = u_r, advance(u_r, before_r, force_r, inverse_r)
 
@@ -434,17 +454,12 @@
     force_m = with_edge(main_force(u, rim, coefs_m), end_force(u_l, rim_l, coefs_l))
     force_r = with_edge(main_force(u_r, far_rim, coefs_r), end_force(u, rim, coefs_m))
     before, u = u, advance(u, before, force_m, inverse_m)
+    u_l = advance(u_l, before_l, main_force(u_l, rim_l, coefs_l), inverse_l)
     u_r = advance(u_r, before_r, force_r, inverse_r)
 
-    rim = first_column(u_r)
-    force_out[...] = end_force(u, rim, coefs_m)
-    pl.when(has_right)(lambda: force_copy().start())
-    force_m = main_force(u, rim, coefs_m)
-    for h in range(1, q_groups):
-        adj_far(h).wait_recv()
-        adj_near(h).start()
-    pl.when(has_left)(lambda: force_copy().wait_recv())
-    u = advance(u, before, with_edge(force_m, force_in[...]), inverse_m)
+    rim_l, rim = first_column(u), first_column(u_r)
+    force_m = with_edge(main_force(u, rim, coefs_m), end_force(u_l, rim_l, coefs_l))
+    u = advance(u, before, force_m, inverse_m)
 
     for a in range(nr):
         gathered[o, :, a * cols : (a + 1) * cols, :] = u[a]
@@ -462,6 +477,9 @@
 
     pl.loop(1, groups)(lambda h: far(h).start())
     near(0).start()
+    for h in range(1, q_groups):
+        adj_far(h).wait_recv()
+        adj_near(h).start()
     for a in range(nr):
         out_u[:, a] = u[a]
 
@@ -574,7 +592,7 @@
     pl.when(has_right)(lambda: to_right().wait_send())
     pl.loop(1, n)(lambda h: meta_copy(h).wait_send())
     pl.when(has_left_2)(lambda: to_left_2().wait_send())
-    pl.when(has_right)(lambda: force_copy().wait_send())
+    pl.when(has_right_2)(lambda: to_right_2().wait_send())
     for h in range(q_groups):
         adj_near(h).wait_send()
         if h:
@@ -628,7 +646,7 @@
             buf(*tiles.shape),
             buf(2 * comps * nr + 2, cols, width), buf(2, 2 * comps * nr + 2, cols, width),
             buf(2 * comps, cols, width), buf(2 * comps, cols, width),
-            buf(comps, cols, width), buf(comps, cols, width),
+            buf((comps * nr + 1) // 2 + 2, cols, width), buf((comps * nr + 1) // 2 + 2, cols, width),
             buf(n, 8, width), buf(n, comps, slot, width), buf(n // 2 + 1, 3 * cells, width),
             buf(az, 9, cells, phi_width),
             buf(az, cells, phi_width), buf(az, cells, phi_width),

time: 34.9 us -> 32 us (0.917)
  Pallas kernels: 32.9 us -> 29.9 us
    pallas_call x1, Pallas kernels: 32.9 us -> 29.9 us  [on_device(): pl.pallas_call(functools.partial(kernel, n, az), out_shape=(pltpu.VMEM(di...]
where the time goes in v5:
time: 32 us; the launch traced here: 31.8 us
  Pallas kernels  29.9 us (93%)
  local copies, waits for them, and re-layouts  1.23 us (4%)
  between operations  0.64 us (2%)
    pallas_call x1, Pallas kernels, on_device(): pl.pallas_call(functools.partial(kernel, n, az), out_shape=(pltpu.VMEM(di...  29.9 us
    unnamed x2, local copies, waits for them, and re-layouts  1.23 us

profile of v5, /device:TPU:0, one launch (start us, length us, event | category | flops | bytes accessed | tf_op | source)
XLA Modules:
  0.0 31.8 jit_solution(13009306281651924266)
XLA Ops:
  0.6 29.9 %shard_map.158 = (f32[3,5,8,128]{3,2,1,0:T(8,128)S(1)}, f32[32,128]{1,0:T(8,128)S(1)}) custom-call(f32[15,8,128]{2,1,0:T(8,128)} %bitcast.11, f32[15,8,128]{2,1,0:T(8,128)} %bitcast.12, f32[1,2]{1,0:T(1,128)} %modulus_a.1, f32[1,2]{1,0:T(1,128)} %hoop_a.1, f32[1,2]{1,0:T(1,128)} %coupling_a.1, f32[1,2]{1,0:T(1,128)} %density_a.1, s32[1,2]{1,0:T(1,128)} %orders_a.1, ...), custom_call_target="tpu_custom_call" | custom-call | tf_op jit(solution)/shard_map/pallas_call | solution.py:634
  30.6 0.6 %copy.19 = f32[3,5,8,128]{3,2,1,0:T(8,128)} copy(f32[3,5,8,128]{3,2,1,0:T(8,128)S(1)} %get-tuple-element.6) | data formatting | bytes 122880
  31.2 0.6 %copy.20 = f32[8,4,128]{2,1,0:T(4,128)} copy(f32[8,4,128]{2,1,0:T(4,128)S(1)} %bitcast.9) | data formatting | bytes 32768
